TPU v7x, 256 devices: a whole 4x4x8 slice. The times are simulated.
256 devices in a mesh: pair: 8 (over x, core), virt: 32 (over y, z).
Axes of the slice: x: 4, y: 4, z: 8, core: 2. Of those that a mesh axis runs over, the one named last changes fastest.
Arguments:
- amplitudes: bfloat16 [640, 320, 320], P('pair', 'virt'), may hold values from -6 to 6
- integrals: bfloat16 [320, 320, 16, 320], P('virt', 'pair'), may hold values from -0.109375 to 0.109375
- virt_irrep: int32 [320], replicated, may hold values from 0 to 7
- tile_irrep: int32 [16], replicated, may hold values from 0 to 7
- pair_irrep: int32 [640], replicated, may hold values from 0 to 7
Outputs:
- ladder: float32 [640, 16, 320], P('pair', None, 'virt')
All inputs are finite; a program needn't handle non-finite values.
Results may differ from a plain program's by a relative error of at most 0.0003.
Values may be sent and summed in bfloat16 or wider, within the bound.
No kernel may reach another device: no remote copies, remote signals or barrier semaphores. Data moves between devices by JAX's collectives and lax.ppermute only.
A program may use at most 128 MiB of HBM per device.

v0:
```python
import jax
import jax.numpy as jnp
from jax import lax
from jax.sharding import PartitionSpec as P


def body(amplitudes, integrals, virt_irrep, tile_irrep, pair_irrep):
    pair_rows = amplitudes.shape[0]
    own_c = integrals.shape[0]
    own_d = integrals.shape[1]
    tile_len = integrals.shape[2]
    full_width = integrals.shape[3]
    pair_count = pair_irrep.shape[0]
    c_labels = lax.dynamic_slice_in_dim(virt_irrep, lax.axis_index("virt") * own_c, own_c)
    d_labels = lax.dynamic_slice_in_dim(virt_irrep, lax.axis_index("pair") * own_d, own_d)
    local_pairs = lax.dynamic_slice_in_dim(
        pair_irrep, lax.axis_index("pair") * pair_rows, pair_rows
    )
    amp_sym = jnp.bitwise_xor(c_labels[:, None], virt_irrep[None, :])
    amp_keep = amp_sym[None] == local_pairs[:, None, None]
    masked_amp = jnp.where(amp_keep, amplitudes, jnp.zeros_like(amplitudes))
    cd_sym = jnp.bitwise_xor(c_labels[:, None], d_labels[None, :])
    ab_sym = jnp.bitwise_xor(tile_irrep[:, None], virt_irrep[None, :])
    int_keep = cd_sym[:, :, None, None] == ab_sym[None, None]
    masked_int = jnp.where(int_keep, integrals, jnp.zeros_like(integrals))
    amp_pairs = lax.all_to_all(masked_amp, "pair", split_axis=2, concat_axis=0, tiled=True)
    flat_amp = amp_pairs.reshape(pair_count, own_c * own_d)
    flat_int = masked_int.reshape(own_c * own_d, tile_len * full_width)
    partial_value = jnp.dot(flat_amp, flat_int, preferred_element_type=jnp.float32)
    partial_value = partial_value.reshape(pair_count, tile_len, full_width)
    summed = lax.psum_scatter(partial_value, "virt", scatter_dimension=2, tiled=True)
    return lax.psum_scatter(summed, "pair", scatter_dimension=0, tiled=True)


def solution(mesh):
    in_specs = (P("pair", "virt", None), P("virt", "pair", None, None), P(), P(), P())
    out_specs = P("pair", None, "virt")
    return jax.shard_map(body, mesh=mesh, in_specs=in_specs, out_specs=out_specs, check_vma=False)
```

profile of v0, /device:TPU:6, one launch (start us, length us, event | category | flops | bytes accessed | tf_op | source)
XLA Modules:
  0.0 355.9 jit_solution(5939161159741101852)
XLA Ops:
  6.5 0.0 copy-start
  6.5 0.0 copy-start.1
  6.5 0.8 dynamic_slice.9
  7.4 0.8 broadcast_xor_fusion
  8.2 3.1 copy.12
  11.3 0.8 dynamic_slice.10
  12.0 1.0 fusion
  13.0 2.1 reshape.93
  15.2 5.6 %all-to-all-start = ((bf16[8,2,16000]{2,1,0:T(2,128)(2,1)}), bf16[8,2,16000]{2,1,0:T(2,128)(2,1)S(1)}, u32[]{:S(2)}, u32[]{:S(2)}) async-start(bf16[8,2,16000]{2,1,0:T(2,128)(2,1)} %reshape.93), calls=%async_computation | async-start | bytes 1024000 | tf_op jit(solution)/shard_map/all_to_all | solution.py:26
  20.8 0.0 reduce-scatter.5.cloned.1.call-start
  20.8 0.0 copy-done
  20.8 0.1 dynamic_slice.11
  20.9 0.1 broadcast_xor_fusion.2
  21.0 0.0 copy-done.1
  21.0 0.1 broadcast_xor_fusion.1
  21.1 4.7 %compare_select_fusion = bf16[10,40,16,320]{3,2,1,0:T(8,128)(2,1)} fusion(bf16[10,40,16,320]{3,2,1,0:T(8,128)(2,1)} %param.6, s32[16,320]{1,0:T(8,128)S(1)} %broadcast_xor_fusion.1, s32[10,40]{1,0:T(8,128)S(1)} %broadcast_xor_fusion.2), kind=kLoop, calls=%fused_computation | loop fusion | flops 4096000 | bytes 8214080 | tf_op jit(solution)/shard_map/jit(_where)/select_n | solution.py:25
  25.7 8.8 %reshape.88 = bf16[400,5120]{1,0:T(8,128)(2,1)} reshape(bf16[10,40,16,320]{3,2,1,0:T(8,128)(2,1)} %compare_select_fusion) | data formatting | bytes 8192000 | tf_op jit(solution)/shard_map/reshape | solution.py:28
  34.5 8.9 %dot_general.8 = bf16[16,320,400]{1,0,2:T(8,128)(2,1)} reshape(bf16[5120,400]{0,1:T(8,128)(2,1)} %bitcast.18) | data formatting | bytes 8192000 | tf_op jit(solution)/shard_map/dot_general | solution.py:29
  43.4 9.3 %copy.19 = bf16[16,320,400]{2,0,1:T(8,128)(2,1)} copy(bf16[16,320,400]{1,0,2:T(8,128)(2,1)} %dot_general.8) | data formatting | bytes 8192000 | tf_op jit(solution)/shard_map/dot_general | solution.py:29
  52.7 0.0 all-to-all-done
  52.7 1.5 reshape.94
  54.2 0.5 copy.14
  54.8 0.6 reshape.89
  55.4 11.4 %fusion.1 = f32[640,16,320]{0,1,2:T(8,128)} fusion(bf16[640,400,1]{0,1,2:T(8,128)(2,1)S(1)} %reshape.89, bf16[16,320,400]{2,0,1:T(8,128)(2,1)} %copy.19), kind=kOutput, calls=%fused_computation.6 | convolution fusion | flops 2621440000 | bytes 17715200 | tf_op jit(solution)/shard_map/dot_general | solution.py:29
  66.8 0.0 reduce-scatter.5.cloned.1.call-update
  66.8 0.3 reduce-scatter.7.cloned.1.call-start
  67.1 241.1 %reduce-scatter.5.cloned.1.call-done = f32[640,16,10]{0,1,2:T(8,128)} async-done(((f32[640,16,320]{0,1,2:T(8,128)}), f32[640,16,10]{0,1,2:T(8,128)}) %reduce-scatter.5.cloned.1.call-update) | async-done | bytes 409616 | tf_op jit(solution)/shard_map/reduce_scatter | solution.py:31
  308.2 4.1 %copy.23 = f32[640,16,10]{2,1,0:T(8,128)} copy(f32[640,16,10]{0,1,2:T(8,128)} %reduce-scatter.5.cloned.1.call-done) | data formatting | bytes 819200
  312.3 5.3 %reshape.91 = f32[640,160]{1,0:T(8,128)} reshape(f32[640,16,10]{2,1,0:T(8,128)} %copy.23) | data formatting | bytes 819200
  317.5 0.0 reduce-scatter.7.cloned.1.call-update
  317.6 29.3 %reduce-scatter.7.cloned.1.call-done = f32[80,160]{1,0:T(8,128)} async-done(((f32[640,160]{1,0:T(8,128)}), f32[80,160]{1,0:T(8,128)}) %reduce-scatter.7.cloned.1.call-update) | async-done | bytes 51216
  346.8 1.3 reshape.92
  348.1 1.0 copy.18
Async XLA Ops:
  6.5 14.3 %copy-start = (s32[320]{0:T(512)S(1)}, s32[320]{0:T(512)}, u32[]{:S(2)}) copy-start(s32[320]{0:T(512)} %param.7) | copy-start | bytes 3844
  6.5 14.4 %copy-start.1 = (s32[16]{0:T(128)S(1)}, s32[16]{0:T(128)}, u32[]{:S(2)}) copy-start(s32[16]{0:T(128)} %param.8) | copy-start | bytes 196
  15.2 37.5 %all-to-all-start = ((bf16[8,2,16000]{2,1,0:T(2,128)(2,1)}), bf16[8,2,16000]{2,1,0:T(2,128)(2,1)S(1)}, u32[]{:S(2)}, u32[]{:S(2)}) async-start(bf16[8,2,16000]{2,1,0:T(2,128)(2,1)} %reshape.93), calls=%async_computation | async-start | bytes 1024000 | tf_op jit(solution)/shard_map/all_to_all | solution.py:26
  20.8 287.4 %reduce-scatter.5.cloned.1.call-start = ((), (), s32[]{:S(2)}) async-start(), calls=%async_computation.3 | async-start | bytes 13516800 | tf_op jit(solution)/shard_map/reduce_scatter | solution.py:31
  66.8 280.1 %reduce-scatter.7.cloned.1.call-start = ((), (), s32[]{:S(2)}) async-start(), calls=%async_computation.4 | async-start | bytes 737280
Sparse Core Ops, SparseCore 0:
  66.9 241.2 reduce-scatter.4
  317.7 29.1 reduce-scatter.6
where the time goes:
time: 360 us; the launch traced here: 356 us
  waiting for transfers between devices  270 us (75%)
  local copies, waits for them, and re-layouts  48.1 us (13%)
  between operations  13.5 us (4%)
  matrix products  11.4 us (3%)
  other arithmetic  6.6 us (2%)
  starting transfers between devices  5.9 us (2%)
    reduce_scatter x1, waiting for transfers between devices, body(): lax.psum_scatter(partial_value, 'virt', scatter_dimension=2, tiled=True)  241 us
    unnamed x3, waiting for transfers between devices  29.3 us
    dot_general x2, local copies, waits for them, and re-layouts, body(): jnp.dot(flat_amp, flat_int, preferred_element_type=jnp.float32)  18.2 us
    unnamed x10, local copies, waits for them, and re-layouts  17.4 us
    dot_general x1, matrix products, body(): jnp.dot(flat_amp, flat_int, preferred_element_type=jnp.float32)  11.4 us
    reshape x1, local copies, waits for them, and re-layouts, body(): flat_int = masked_int.reshape(own_c * own_d, tile_len * full_width)  8.79 us
  transfers between devices with their start and end apart: 3, of which 2 were waited for; matrix products, arithmetic and copies ran while one was open for 9% of the time, Pallas kernels for 0%

commit v1 on v0

v1 whole, which is shorter than its diff:
```python
import functools

import jax
import jax.numpy as jnp
from jax import lax
from jax.experimental import pallas as pl
from jax.experimental.pallas import tpu as pltpu
from jax.sharding import PartitionSpec as P

F32 = jnp.float32
BF16 = jnp.bfloat16
I32 = jnp.int32
SLOTS = 24
CHIPS = 4
CORES = 2
OWNERS = CHIPS * CORES
COLUMNS = 32
ROWS = 80
OWN_C = 10
OWN_D = 40
OWN_A = 10
TILE = 16
HALF = TILE // 2
WIDTH = 320
DEPTH = OWN_C * OWN_D
DEPTH_PAD = 512
WORDS = HALF * WIDTH
MESSAGE = WORDS + 128
CORE_ROWS = CHIPS * SLOTS
FINE = 64.0
FULL = 32767.0
VMEM = pl.BlockSpec(memory_space=pltpu.VMEM)
SMEM = pl.BlockSpec(memory_space=pltpu.SMEM)


def params():
    return pltpu.CompilerParams(vmem_limit_bytes=40 * 1024 * 1024)


def iota(shape, axis):
    return lax.broadcasted_iota(I32, shape, axis)


def local_labels(pairs_ref):
    owner = lax.axis_index("pair")
    row = pairs_ref[:, 0:ROWS]
    for k in range(1, OWNERS):
        row = jnp.where(owner == k, pairs_ref[:, k * ROWS : (k + 1) * ROWS], row)
    return row


def slots_of(row, round_index):
    first, second = iota((ROWS, ROWS), 0), iota((ROWS, ROWS), 1)
    spread = jnp.broadcast_to(row.astype(F32), (ROWS, ROWS))
    column = jnp.sum(jnp.where(first == second, spread, 0.0), axis=1, keepdims=True)
    before = (column == spread) & (first < second)
    rank = jnp.sum(jnp.where(before, 1.0, 0.0), axis=0, keepdims=True)
    slot = rank - (round_index * SLOTS).astype(F32)
    hot = iota((SLOTS, ROWS), 0).astype(F32) == slot
    return column, jnp.where(hot, 1.0, 0.0)


def pack_kernel(round_ref, virt_s, virt_v, pairs_v, amp_ref, out_ref, wide):
    row = local_labels(pairs_v)
    column, hot = slots_of(row, round_ref[0])
    hot = hot.astype(BF16)
    column = column.astype(I32)
    base = lax.axis_index("virt") * OWN_C
    wide[:, :, 384:DEPTH_PAD] = jnp.zeros((OWNERS, SLOTS, DEPTH_PAD - 384), F32)
    for c in range(OWN_C):
        key = jnp.bitwise_xor(virt_v[...], virt_s[base + c])
        kept = jnp.where(column == key, amp_ref[c].astype(F32), 0.0).astype(BF16)
        packed = jnp.dot(hot, kept, preferred_element_type=F32)
        for owner in range(OWNERS):
            wide[owner, :, c * OWN_D : (c + 1) * OWN_D] = packed[:, owner * OWN_D : (owner + 1) * OWN_D]
    out_ref[...] = wide[...].astype(BF16)


def tile_column(tile_s):
    column = jnp.zeros((TILE, 1), I32)
    place = iota((TILE, 1), 0)
    for b in range(TILE):
        column = jnp.where(place == b, tile_s[b], column)
    return column


def mask_kernel(virt_s, tile_s, virt_v, int_ref, out_ref, masks, turn):
    step = pl.program_id(0)

    @pl.when(step == 0)
    def _():
        label = jnp.bitwise_xor(tile_column(tile_s), virt_v[...])
        for g in range(8):
            masks[g] = jnp.where(label == g, 1.0, 0.0).astype(BF16)
        high, low = iota((256, 256), 0), iota((256, 256), 1)
        match = (high // 16 == low % 16) & (high % 16 == low // 16)
        turn[...] = jnp.where(match, 1.0, 0.0).astype(BF16)

    base_c = lax.axis_index("virt") * OWN_C + step * 2
    base_d = lax.axis_index("pair") * OWN_D
    for group in range(5):
        slabs = []
        for k in range(16):
            c, d = divmod(group * 16 + k, OWN_D)
            g = jnp.bitwise_xor(virt_s[base_c + c], virt_s[base_d + d])
            slabs.append(int_ref[c, d] * masks[g])
        turned = jnp.dot(turn[...], jnp.concatenate(slabs, axis=0), preferred_element_type=F32).astype(BF16)
        for b in range(TILE):
            out_ref[b, group * 16 : (group + 1) * 16, :] = turned[b * 16 : (b + 1) * 16]


def left_rows(amp_ref, core, left):
    for x in range(CHIPS):
        left[x * SLOTS : (x + 1) * SLOTS, :] = amp_ref[2 * x + core].astype(F32)
    return left[...].astype(BF16)[:, :DEPTH]


def scale_code(largest):
    return jnp.ceil(FINE * jnp.log2(jnp.maximum(largest, 1e-36))).astype(I32)


def scale_up(code):
    return FULL * jnp.exp2(code.astype(F32) * (-1.0 / FINE))


def scale_down(code):
    return jnp.exp2(code.astype(F32) * (1.0 / FINE)) * (1.0 / FULL)


def joined(high, low, factor):
    high = jnp.round(high * factor).astype(I32)
    low = jnp.round(low * factor).astype(I32)
    return jnp.left_shift(high, 16) | (low & 0xFFFF)


def high_of(word):
    return jnp.right_shift(word, 16).astype(F32)


def low_of(word):
    return jnp.right_shift(jnp.left_shift(word, 16), 16).astype(F32)


def row_largest(values):
    top = jnp.abs(values[0])
    for b in range(1, TILE):
        top = jnp.maximum(top, jnp.abs(values[b]))
    return jnp.max(top, axis=1, keepdims=True)


def write_words(values, out_ref):
    code = scale_code(row_largest(values))
    factor = scale_up(code)
    for b in range(HALF):
        out_ref[:, b * WIDTH : (b + 1) * WIDTH] = joined(values[b], values[b + HALF], factor)
    out_ref[:, WORDS:MESSAGE] = jnp.broadcast_to(code, (code.shape[0], MESSAGE - WORDS))


def send_kernel(amp_ref, int_ref, out_ref, left, values):
    other = 1 - lax.axis_index("pair") % CORES
    rows = left_rows(amp_ref, other, left)
    for b in range(TILE):
        values[b] = jnp.dot(rows, int_ref[b], preferred_element_type=F32)
    write_words(values, out_ref)


def keep_kernel(amp_ref, int_ref, out_ref, left):
    rows = left_rows(amp_ref, lax.axis_index("pair") % CORES, left)
    for b in range(TILE):
        out_ref[b] = jnp.dot(rows, int_ref[b], preferred_element_type=F32)


def add_words(words, values, start):
    factor = scale_down(words[:, WORDS : WORDS + 1])
    for b in range(HALF):
        word = words[:, b * WIDTH : (b + 1) * WIDTH]
        values[b] = start[b] + high_of(word) * factor
        values[b + HALF] = start[b + HALF] + low_of(word) * factor


def chip_kernel(keep_ref, got_ref, own_ref, one_ref, two_ref, three_ref, values, words):
    add_words(got_ref, values, keep_ref)
    write_words(values, words)
    x = lax.axis_index("pair") // CORES
    for hop, out in ((1, one_ref), (2, two_ref), (3, three_ref)):
        start = pl.multiple_of(lax.rem(x + hop, CHIPS) * SLOTS, 8)
        out[...] = words[pl.ds(start, SLOTS), :]
    start = pl.multiple_of(x * SLOTS, 8)
    for b in range(TILE):
        own_ref[b] = values[b, pl.ds(start, SLOTS), :]


def piece(group, b):
    index = group * HALF + b
    return 8 * (index // 12), OWN_A * (index % 12)


def column_kernel(own_ref, one_ref, two_ref, three_ref, out_ref, values, words):
    add_words(one_ref, values, own_ref)
    add_words(two_ref, values, values)
    add_words(three_ref, values, values)
    write_words(values, words)
    code = words[:, WORDS : WORDS + 8]
    lane = iota((8, 8), 1)
    tail = jnp.where(lane == 0, code[0:8], jnp.where(lane == 1, code[8:16], code[16:24]))
    for j in range(COLUMNS):
        for group in range(SLOTS // 8):
            for b in range(HALF):
                row, lane_at = piece(group, b)
                start = b * WIDTH + j * OWN_A
                out_ref[j, row : row + 8, lane_at : lane_at + OWN_A] = words[
                    group * 8 : group * 8 + 8, start : start + OWN_A
                ]
        out_ref[j, 0:8, 120:128] = tail
        out_ref[j, 8:16, 120:128] = tail


def final_kernel(round_ref, virt_s, tile_s, pairs_v, got_ref, out_ref, flat):
    row = local_labels(pairs_v)
    _, hot = slots_of(row, round_ref[0])
    lane = iota((8, 128), 1)
    sums = [[jnp.zeros((8, 128), F32) for _ in range(2)] for _ in range(2)]
    for j in range(COLUMNS):
        for block in range(2):
            word = got_ref[j, 8 * block : 8 * block + 8, :]
            if block == 0:
                code = jnp.where(lane < 80, word[:, 120:121], word[:, 121:122])
            else:
                code = jnp.where(lane < 40, word[:, 121:122], word[:, 122:123])
            factor = scale_down(code)
            sums[0][block] += high_of(word) * factor
            sums[1][block] += low_of(word) * factor
    for half in range(2):
        for group in range(SLOTS // 8):
            for b in range(HALF):
                at, lane_at = piece(group, b)
                to = (half * HALF + b) * OWN_A
                flat[group * 8 : group * 8 + 8, to : to + OWN_A] = sums[half][at // 8][:, lane_at : lane_at + OWN_A]
    spread = lax.dot_general(
        flat[...], hot, (((0,), (0,)), ((), ())), precision=lax.Precision.HIGHEST, preferred_element_type=F32
    )
    base = lax.axis_index("virt") * OWN_A
    column = tile_column(tile_s)
    for a in range(OWN_A):
        for b in range(TILE):
            out_ref[a, b : b + 1, :] = spread[b * OWN_A + a : b * OWN_A + a + 1]
        keep = jnp.bitwise_xor(column, virt_s[base + a]) == row
        out_ref[a] = jnp.where(keep, out_ref[a], 0.0)


def shape(dims, dtype):
    return jax.ShapeDtypeStruct(dims, dtype)


def masked_integrals(integrals, virt, tile, virt_row):
    return pl.pallas_call(
        mask_kernel,
        out_shape=shape((TILE, DEPTH, WIDTH), BF16),
        grid=(OWN_C // 2,),
        in_specs=[
            SMEM,
            SMEM,
            pl.BlockSpec((1, WIDTH), lambda s: (0, 0)),
            pl.BlockSpec((2, OWN_D, TILE, WIDTH), lambda s: (s, 0, 0, 0)),
        ],
        out_specs=pl.BlockSpec((TILE, 2 * OWN_D, WIDTH), lambda s: (0, s, 0)),
        scratch_shapes=[pltpu.VMEM((8, TILE, WIDTH), BF16), pltpu.VMEM((256, 256), BF16)],
        compiler_params=params(),
        name="mask_turn",
        cost_estimate=pl.CostEstimate(flops=1 << 30, bytes_accessed=10 << 20, transcendentals=0),
    )(virt, tile, virt_row, integrals)


def one_round(round_index, amplitudes, integrals, virt, tile, pairs):
    virt_row = virt.reshape(1, WIDTH)
    pair_row = pairs.reshape(1, OWNERS * ROWS)
    number = jnp.reshape(round_index, (1,)).astype(I32)
    packed = pl.pallas_call(
        pack_kernel,
        out_shape=shape((OWNERS, SLOTS, DEPTH_PAD), BF16),
        in_specs=[SMEM, SMEM, VMEM, VMEM, VMEM],
        out_specs=VMEM,
        scratch_shapes=[pltpu.VMEM((OWNERS, SLOTS, DEPTH_PAD), F32)],
        compiler_params=params(),
        name="pack",
    )(number, virt, virt_row, pair_row, jnp.transpose(amplitudes, (1, 0, 2)))
    amp = lax.all_to_all(packed, "pair", split_axis=0, concat_axis=0, tiled=True)
    ints = masked_integrals(integrals, virt, tile, virt_row)
    left = pltpu.VMEM((CORE_ROWS, DEPTH_PAD), F32)
    table = pltpu.VMEM((TILE, CORE_ROWS, WIDTH), F32)
    send = pl.pallas_call(
        send_kernel,
        out_shape=shape((CORE_ROWS, MESSAGE), I32),
        in_specs=[VMEM, VMEM],
        out_specs=VMEM,
        scratch_shapes=[left, table],
        compiler_params=params(),
        name="send_rows",
    )(amp, ints)
    got = lax.ppermute(send, "pair", [(i, i ^ 1) for i in range(OWNERS)])
    keep = pl.pallas_call(
        keep_kernel,
        out_shape=shape((TILE, CORE_ROWS, WIDTH), F32),
        in_specs=[VMEM, VMEM],
        out_specs=VMEM,
        scratch_shapes=[left],
        compiler_params=params(),
        name="keep_rows",
        cost_estimate=pl.CostEstimate(flops=1 << 29, bytes_accessed=8 << 20, transcendentals=0),
    )(amp, ints)
    own, one, two, three = pl.pallas_call(
        chip_kernel,
        out_shape=[shape((TILE, SLOTS, WIDTH), F32)] + [shape((SLOTS, MESSAGE), I32)] * 3,
        in_specs=[VMEM, VMEM],
        out_specs=[VMEM] * 4,
        scratch_shapes=[table, pltpu.VMEM((CORE_ROWS, MESSAGE), I32)],
        compiler_params=params(),
        name="chip_sum",
    )(keep, got)
    hops = [
        lax.ppermute(part, "pair", [(i, (i + CORES * hop) % OWNERS) for i in range(OWNERS)])
        for hop, part in ((1, one), (2, two), (3, three))
    ]
    parts = pl.pallas_call(
        column_kernel,
        out_shape=shape((COLUMNS, 16, 128), I32),
        in_specs=[VMEM] * 4,
        out_specs=VMEM,
        scratch_shapes=[pltpu.VMEM((TILE, SLOTS, WIDTH), F32), pltpu.VMEM((SLOTS, MESSAGE), I32)],
        compiler_params=params(),
        name="column_sum",
    )(own, *hops)
    back = lax.all_to_all(parts, "virt", split_axis=0, concat_axis=0, tiled=True)
    return pl.pallas_call(
        final_kernel,
        out_shape=shape((OWN_A, TILE, ROWS), F32),
        in_specs=[SMEM, SMEM, SMEM, VMEM, VMEM],
        out_specs=VMEM,
        scratch_shapes=[pltpu.VMEM((SLOTS, TILE * OWN_A), F32)],
        compiler_params=params(),
        name="unpack",
    )(number, virt, tile, pair_row, back)


def body(amplitudes, integrals, virt_irrep, tile_irrep, pair_irrep):
    run = functools.partial(
        one_round,
        amplitudes=amplitudes,
        integrals=integrals,
        virt=virt_irrep,
        tile=tile_irrep,
        pairs=pair_irrep,
    )
    counts = jnp.sum(
        (pair_irrep.reshape(OWNERS, ROWS)[:, :, None] == jnp.arange(8)).astype(I32), axis=1
    )
    rounds = (jnp.max(counts) + SLOTS - 1) // SLOTS
    first = run(jnp.zeros((), I32))
    _, total = lax.while_loop(
        lambda state: state[0] < rounds,
        lambda state: (state[0] + 1, state[1] + run(state[0])),
        (jnp.ones((), I32), first),
    )
    return jnp.transpose(total, (2, 1, 0))


def solution(mesh):
    in_specs = (P("pair", "virt", None), P("virt", "pair", None, None), P(), P(), P())
    out_specs = P("pair", None, "virt")
    return jax.shard_map(body, mesh=mesh, in_specs=in_specs, out_specs=out_specs, check_vma=False)
```

time: 360 us -> 69.6 us (0.19); the launches traced: 356 us -> 69.2 us
  waiting for transfers between devices: 270 us -> 24.8 us
  local copies, waits for them, and re-layouts: 48.1 us -> 4.5 us
  Pallas kernels: 0 us -> 18.5 us
  starting transfers between devices: 5.9 us -> 19.5 us
  between operations: 13.5 us -> 0.82 us
  matrix products: 11.4 us -> 0 us
  other arithmetic: 6.6 us -> 0.85 us
    reduce_scatter x1 -> x0, waiting for transfers between devices: 241 us -> none  [body(): lax.psum_scatter(partial_value, 'virt', scatter_dimension=2, tiled=True)]
    unnamed x3 -> x0, waiting for transfers between devices: 29.3 us -> none
    pallas_call x0 -> x7, Pallas kernels: none -> 18.5 us  [the longest x1 5.37 us: masked_integrals(): pl.pallas_call(mask_kernel, out_shape=shape((TILE, DEPTH, WIDTH), BF16),...]
    dot_general x2 -> x0, local copies, waits for them, and re-layouts: 18.2 us -> none  [body(): jnp.dot(flat_amp, flat_int, preferred_element_type=jnp.float32)]
    unnamed x10 -> x14, local copies, waits for them, and re-layouts: 17.4 us -> 3.05 us
    ppermute x0 -> x4, waiting for transfers between devices: none -> 13.9 us  [the longest x3 12.5 us: one_round(): lax.ppermute(part, 'pair', [(i, (i + CORES * hop) % OWNERS) for i in rang...]
    dot_general x1 -> x0, matrix products: 11.4 us -> none  [body(): jnp.dot(flat_amp, flat_int, preferred_element_type=jnp.float32)]
    all_to_all x1 -> x2, waiting for transfers between devices: 0.01 us -> 10.9 us  [the longest x1 10.9 us: one_round(): lax.all_to_all(parts, 'virt', split_axis=0, concat_axis=0, tiled=True)]
  transfers between devices with their start and end apart: 3 -> 6, of which waited for: 2 -> 5; matrix products, arithmetic and copies ran while one was open for 9% -> 1% of each run, Pallas kernels for 0% -> 9%
where the time goes in v1:
time: 69.6 us; the launch traced here: 69.2 us
  waiting for transfers between devices  24.8 us (36%)
  starting transfers between devices  19.5 us (28%)
  Pallas kernels  18.5 us (27%)
  local copies, waits for them, and re-layouts  4.5 us (6%)
  other arithmetic  0.85 us (1%)
  between operations  0.82 us (1%)
    ppermute x3, waiting for transfers between devices, one_round(): lax.ppermute(part, 'pair', [(i, (i + CORES * hop) % OWNERS) for i in rang...  12.5 us
    all_to_all x1, waiting for transfers between devices, one_round(): lax.all_to_all(parts, 'virt', split_axis=0, concat_axis=0, tiled=True)  10.9 us
    all_to_all x1, starting transfers between devices, one_round(): lax.all_to_all(parts, 'virt', split_axis=0, concat_axis=0, tiled=True)  10.7 us
    all_to_all x1, starting transfers between devices, one_round(): lax.all_to_all(packed, 'pair', split_axis=0, concat_axis=0, tiled=True)  5.54 us
    pallas_call x1, Pallas kernels, masked_integrals(): pl.pallas_call(mask_kernel, out_shape=shape((TILE, DEPTH, WIDTH), BF16),...  5.37 us
    pallas_call x1, Pallas kernels, one_round(): pl.pallas_call(send_kernel, out_shape=shape((CORE_ROWS, MESSAGE), I32), i...  4.01 us
    unnamed x14, local copies, waits for them, and re-layouts  3.05 us
    ppermute x3, starting transfers between devices, one_round(): lax.ppermute(part, 'pair', [(i, (i + CORES * hop) % OWNERS) for i in rang...  3 us
  transfers between devices with their start and end apart: 6, of which 5 were waited for; matrix products, arithmetic and copies ran while one was open for 1% of the time, Pallas kernels for 9%

profile of v1, /device:TPU:6, one launch (start us, length us, event | category | flops | bytes accessed | tf_op | source)
XLA Modules:
  0.0 69.2 jit_solution(11071570380127561442)
XLA Ops:
  0.0 0.7 reshape.17.virt_v
  0.7 0.7 reshape.16.pairs_v
  1.4 3.0 %pack.4 = bf16[8,24,512]{2,1,0:T(8,128)(2,1)} custom-call(s32[1]{0:T(128)} %constant.19.clone.1.round_ref, s32[320]{0:T(512)} %virt_s.5, s32[1,320]{1,0:T(1,128)S(1)} %reshape.17.virt_v, s32[1,640]{1,0:T(1,128)S(1)} %reshape.16.pairs_v, bf16[10,80,320]{2,1,0:T(8,128)(2,1)} %bitcast.10), custom_call_target="tpu_custom_call" | custom-call | tf_op jit(solution)/shard_map/pack/pallas_call | solution.py:278
  4.4 5.5 %all-to-all-start.2 = ((bf16[8,24,512]{2,1,0:T(8,128)(2,1)}), bf16[8,24,512]{2,1,0:T(8,128)(2,1)S(1)}, u32[]{:S(2)}, u32[]{:S(2)}) async-start(bf16[8,24,512]{2,1,0:T(8,128)(2,1)} %pack.4), calls=%async_computation.2 | async-start | bytes 393216 | tf_op jit(solution)/shard_map/all_to_all | solution.py:287
  9.9 0.0 copy-start
  9.9 2.4 %copy-done = bf16[10,40,16,320]{3,2,1,0:T(8,128)(2,1)S(1)} copy-done((bf16[10,40,16,320]{3,2,1,0:T(8,128)(2,1)S(1)}, bf16[10,40,16,320]{3,2,1,0:T(8,128)(2,1)}, u32[]{:S(2)}) %copy-start) | copy-done | bytes 4096024
  12.3 5.4 %mask_turn.2.int_ref = bf16[16,400,320]{2,1,0:T(8,128)(2,1)} custom-call(s32[320]{0:T(512)} %virt_s.5, s32[16]{0:T(128)} %tile_s.3, s32[1,320]{1,0:T(1,128)S(1)} %reshape.17.virt_v, bf16[10,40,16,320]{3,2,1,0:T(8,128)(2,1)S(1)} %copy-done), custom_call_target="tpu_custom_call" | custom-call | flops 1073741824 | bytes 10485760 | tf_op jit(solution)/shard_map/mask_turn/pallas_call | solution.py:256
  17.7 0.0 all-to-all-done.2.amp_ref
  17.7 0.0 copy-start.1
  17.7 4.0 %send_rows.4 = s32[96,2688]{1,0:T(8,128)S(1)} custom-call(bf16[8,24,512]{2,1,0:T(8,128)(2,1)S(1)} %all-to-all-done.2.amp_ref, bf16[16,400,320]{2,1,0:T(8,128)(2,1)} %mask_turn.2.int_ref), custom_call_target="tpu_custom_call" | custom-call | tf_op jit(solution)/shard_map/send_rows/pallas_call | solution.py:291
  21.7 0.0 copy-start.6
  21.7 0.0 copy-start.5
  21.7 0.0 copy-start.7
  21.7 0.0 copy-start.3
  21.7 0.2 collective-permute-start.4
  22.0 0.0 copy-done.1
  22.0 1.0 %keep_rows.2.keep_ref = f32[16,96,320]{2,1,0:T(8,128)S(1)} custom-call(bf16[8,24,512]{2,1,0:T(8,128)(2,1)S(1)} %all-to-all-done.2.amp_ref, bf16[16,400,320]{2,1,0:T(8,128)(2,1)S(1)} %copy-done.1), custom_call_target="tpu_custom_call" | custom-call | flops 536870912 | bytes 8388608 | tf_op jit(solution)/shard_map/keep_rows/pallas_call | solution.py:301
  23.0 1.4 %collective-permute-done.4.got_ref = s32[96,2688]{1,0:T(8,128)S(1)} collective-permute-done((s32[96,2688]{1,0:T(8,128)S(1)}, s32[96,2688]{1,0:T(8,128)S(1)}, u32[]{:S(2)}, u32[]{:S(2)}) %collective-permute-start.4) | collective-permute-done | bytes 1032224 | tf_op jit(solution)/shard_map/ppermute | solution.py:300
  24.4 1.1 %chip_sum.4 = (f32[16,24,320]{2,1,0:T(8,128)S(1)}, s32[24,2688]{1,0:T(8,128)S(1)}, s32[24,2688]{1,0:T(8,128)S(1)}, s32[24,2688]{1,0:T(8,128)S(1)}) custom-call(f32[16,96,320]{2,1,0:T(8,128)S(1)} %keep_rows.2.keep_ref, s32[96,2688]{1,0:T(8,128)S(1)} %collective-permute-done.4.got_ref), custom_call_target="tpu_custom_call" | custom-call | tf_op jit(solution)/shard_map/chip_sum/pallas_call | solution.py:311
  25.5 0.2 collective-permute-start.5
  25.7 2.8 %collective-permute-start.6 = (s32[24,2688]{1,0:T(8,128)S(1)}, s32[24,2688]{1,0:T(8,128)S(1)}, u32[]{:S(2)}, u32[]{:S(2)}) collective-permute-start(s32[24,2688]{1,0:T(8,128)S(1)} %get-tuple-element.108), channel_id=1, source_target_pairs={{0,128},{32,160},{64,192},{96,224},{128,0},{160,32},{192,64},{224,... | collective-permute-start | bytes 774152 | tf_op jit(solution)/shard_map/ppermute | solution.py:321
  28.5 0.0 collective-permute-start.7
  28.5 6.1 %collective-permute-done.5.one_ref = s32[24,2688]{1,0:T(8,128)S(1)} collective-permute-done((s32[24,2688]{1,0:T(8,128)S(1)}, s32[24,2688]{1,0:T(8,128)S(1)}, u32[]{:S(2)}, u32[]{:S(2)}) %collective-permute-start.5) | collective-permute-done | bytes 258080 | tf_op jit(solution)/shard_map/ppermute | solution.py:321
  34.7 1.7 %collective-permute-done.6.two_ref = s32[24,2688]{1,0:T(8,128)S(1)} collective-permute-done((s32[24,2688]{1,0:T(8,128)S(1)}, s32[24,2688]{1,0:T(8,128)S(1)}, u32[]{:S(2)}, u32[]{:S(2)}) %collective-permute-start.6) | collective-permute-done | bytes 258080 | tf_op jit(solution)/shard_map/ppermute | solution.py:321
  36.4 4.7 %collective-permute-done.7.three_ref = s32[24,2688]{1,0:T(8,128)S(1)} collective-permute-done((s32[24,2688]{1,0:T(8,128)S(1)}, s32[24,2688]{1,0:T(8,128)S(1)}, u32[]{:S(2)}, u32[]{:S(2)}) %collective-permute-start.7) | collective-permute-done | bytes 258080 | tf_op jit(solution)/shard_map/ppermute | solution.py:321
  41.0 2.4 %column_sum.4 = s32[32,16,128]{2,1,0:T(8,128)} custom-call(f32[16,24,320]{2,1,0:T(8,128)S(1)} %get-tuple-element.106.own_ref, s32[24,2688]{1,0:T(8,128)S(1)} %collective-permute-done.5.one_ref, s32[24,2688]{1,0:T(8,128)S(1)} %collective-permute-done.6.two_ref, s32[24,2688]{1,0:T(8,128)S(1)} %collective-permute-done.7.three_ref), custom_call_target="tpu_custom_call" | custom-call | tf_op jit(solution)/shard_map/column_sum/pallas_call | solution.py:324
  43.4 10.7 %all-to-all-start.3 = ((s32[32,16,128]{2,1,0:T(8,128)}), s32[32,16,128]{2,1,0:T(8,128)S(1)}, u32[]{:S(2)}, u32[]{:S(2)}) async-start(s32[32,16,128]{2,1,0:T(8,128)} %column_sum.4), calls=%async_computation.3 | async-start | bytes 524288 | tf_op jit(solution)/shard_map/all_to_all | solution.py:333
  54.1 0.0 copy-done.6
  54.1 0.1 eq.15
  54.2 0.2 convert_reduce_fusion
  54.4 0.6 reduce_max.9
  55.7 0.0 copy-done.5
  55.8 10.9 %all-to-all-done.3.got_ref = s32[32,16,128]{2,1,0:T(8,128)S(1)} async-done(((s32[32,16,128]{2,1,0:T(8,128)}), s32[32,16,128]{2,1,0:T(8,128)S(1)}, u32[]{:S(2)}, u32[]{:S(2)}) %all-to-all-start.3) | async-done | bytes 262176 | tf_op jit(solution)/shard_map/all_to_all | solution.py:333
  66.7 0.0 copy-done.7
  66.7 1.7 %unpack.4 = f32[10,16,80]{2,1,0:T(8,128)S(1)} custom-call(s32[1]{0:T(128)} %constant.19.clone.1.round_ref, s32[320]{0:T(512)S(1)} %copy-done.5, s32[16]{0:T(128)S(1)} %copy-done.7, s32[1,640]{1,0:T(1,128)S(1)} %reshape.16.pairs_v, s32[32,16,128]{2,1,0:T(8,128)S(1)} %all-to-all-done.3.got_ref), custom_call_target="tpu_custom_call" | custom-call | tf_op jit(solution)/shard_map/unpack/pallas_call | solution.py:334
  68.4 0.0 copy-done.3
  68.4 0.2 while.13
  68.6 0.0 copy-start.4
  68.6 0.6 copy-done.4
  (2 shorter events, 0.0 us)
Async XLA Ops:
  4.4 13.3 %all-to-all-start.2 = ((bf16[8,24,512]{2,1,0:T(8,128)(2,1)}), bf16[8,24,512]{2,1,0:T(8,128)(2,1)S(1)}, u32[]{:S(2)}, u32[]{:S(2)}) async-start(bf16[8,24,512]{2,1,0:T(8,128)(2,1)} %pack.4), calls=%async_computation.2 | async-start | bytes 393216 | tf_op jit(solution)/shard_map/all_to_all | solution.py:287
  9.9 2.4 %copy-start = (bf16[10,40,16,320]{3,2,1,0:T(8,128)(2,1)S(1)}, bf16[10,40,16,320]{3,2,1,0:T(8,128)(2,1)}, u32[]{:S(2)}) copy-start(bf16[10,40,16,320]{3,2,1,0:T(8,128)(2,1)} %int_ref.1) | copy-start | bytes 12288004
  17.7 4.3 %copy-start.1 = (bf16[16,400,320]{2,1,0:T(8,128)(2,1)S(1)}, bf16[16,400,320]{2,1,0:T(8,128)(2,1)}, u32[]{:S(2)}) copy-start(bf16[16,400,320]{2,1,0:T(8,128)(2,1)} %mask_turn.2.int_ref) | copy-start | bytes 12288004
  21.7 32.4 %copy-start.6 = (s32[640]{0:T(1024)S(1)}, s32[640]{0:T(1024)}, u32[]{:S(2)}) copy-start(s32[640]{0:T(1024)} %param.11) | copy-start | bytes 7684
  21.7 34.0 %copy-start.5 = (s32[320]{0:T(512)S(1)}, s32[320]{0:T(512)}, u32[]{:S(2)}) copy-start(s32[320]{0:T(512)} %virt_s.5) | copy-start | bytes 3844
  21.7 45.0 %copy-start.7 = (s32[16]{0:T(128)S(1)}, s32[16]{0:T(128)}, u32[]{:S(2)}) copy-start(s32[16]{0:T(128)} %tile_s.3) | copy-start | bytes 196
  21.7 46.6 %copy-start.3 = (bf16[80,10,320]{2,0,1:T(8,128)(2,1)S(1)}, bf16[80,10,320]{2,0,1:T(8,128)(2,1)}, u32[]{:S(2)}) copy-start(bf16[80,10,320]{2,0,1:T(8,128)(2,1)} %param.7) | copy-start | bytes 1536004
  21.7 2.7 %collective-permute-start.4 = (s32[96,2688]{1,0:T(8,128)S(1)}, s32[96,2688]{1,0:T(8,128)S(1)}, u32[]{:S(2)}, u32[]{:S(2)}) collective-permute-start(s32[96,2688]{1,0:T(8,128)S(1)} %send_rows.4), channel_id=1, source_target_pairs={{0,32},{32,0},{64,96},{96,64},{128,160},{160,128},{192,224},{224,1... | collective-permute-start | bytes 3096584 | tf_op jit(solution)/shard_map/ppermute | solution.py:300
  25.5 9.1 %collective-permute-start.5 = (s32[24,2688]{1,0:T(8,128)S(1)}, s32[24,2688]{1,0:T(8,128)S(1)}, u32[]{:S(2)}, u32[]{:S(2)}) collective-permute-start(s32[24,2688]{1,0:T(8,128)S(1)} %get-tuple-element.107), channel_id=1, source_target_pairs={{0,64},{32,96},{64,128},{96,160},{128,192},{160,224},{192,0},{224,... | collective-permute-start | bytes 774152 | tf_op jit(solution)/shard_map/ppermute | solution.py:321
  25.7 10.6 %collective-permute-start.6 = (s32[24,2688]{1,0:T(8,128)S(1)}, s32[24,2688]{1,0:T(8,128)S(1)}, u32[]{:S(2)}, u32[]{:S(2)}) collective-permute-start(s32[24,2688]{1,0:T(8,128)S(1)} %get-tuple-element.108), channel_id=1, source_target_pairs={{0,128},{32,160},{64,192},{96,224},{128,0},{160,32},{192,64},{224,... | collective-permute-start | bytes 774152 | tf_op jit(solution)/shard_map/ppermute | solution.py:321
  28.5 12.5 %collective-permute-start.7 = (s32[24,2688]{1,0:T(8,128)S(1)}, s32[24,2688]{1,0:T(8,128)S(1)}, u32[]{:S(2)}, u32[]{:S(2)}) collective-permute-start(s32[24,2688]{1,0:T(8,128)S(1)} %get-tuple-element.109), channel_id=1, source_target_pairs={{0,192},{32,224},{64,0},{96,32},{128,64},{160,96},{192,128},{224,1... | collective-permute-start | bytes 774152 | tf_op jit(solution)/shard_map/ppermute | solution.py:321
  43.4 23.3 %all-to-all-start.3 = ((s32[32,16,128]{2,1,0:T(8,128)}), s32[32,16,128]{2,1,0:T(8,128)S(1)}, u32[]{:S(2)}, u32[]{:S(2)}) async-start(s32[32,16,128]{2,1,0:T(8,128)} %column_sum.4), calls=%async_computation.3 | async-start | bytes 524288 | tf_op jit(solution)/shard_map/all_to_all | solution.py:333
  68.6 0.6 copy-start.4

commit v2 on v1

v2 whole, which is shorter than its diff:
```python
import functools

import jax
import jax.numpy as jnp
from jax import lax
from jax.experimental import pallas as pl
from jax.experimental.pallas import tpu as pltpu
from jax.sharding import PartitionSpec as P

F32 = jnp.float32
BF16 = jnp.bfloat16
I32 = jnp.int32
SLOTS = 24
CHIPS = 4
CORES = 2
OWNERS = CHIPS * CORES
COLUMNS = 32
ROWS = 80
OWN_C = 10
OWN_D = 40
OWN_A = 10
TILE = 16
HALF = TILE // 2
WIDTH = 320
DEPTH = OWN_C * OWN_D
DEPTH_PAD = 512
WORDS = HALF * WIDTH
MESSAGE = WORDS + 128
CORE_ROWS = CHIPS * SLOTS
HOPS = (2, 1, 3, 0)
REST = CORE_ROWS - SLOTS
FINE = 64.0
FULL = 32767.0
WIDTH_PAD = 384
GROUPS = 2 * OWN_D // 16
PAIRS_B = TILE // 2
PAIR = 2 * WIDTH
NEAR = 6
FAR = PAIRS_B - NEAR
HBM = pl.BlockSpec(memory_space=pltpu.HBM)
VMEM = pl.BlockSpec(memory_space=pltpu.VMEM)
SMEM = pl.BlockSpec(memory_space=pltpu.SMEM)


def params():
    return pltpu.CompilerParams(vmem_limit_bytes=40 * 1024 * 1024)


def iota(shape, axis):
    return lax.broadcasted_iota(I32, shape, axis)


def local_labels(pairs_ref):
    owner = lax.axis_index("pair")
    every = pairs_ref[...].reshape(1, OWNERS * ROWS)
    row = every[:, 0:ROWS]
    for k in range(1, OWNERS):
        row = jnp.where(owner == k, every[:, k * ROWS : (k + 1) * ROWS], row)
    return row


def slots_of(row, round_index):
    first, second = iota((ROWS, ROWS), 0), iota((ROWS, ROWS), 1)
    spread = jnp.broadcast_to(row.astype(F32), (ROWS, ROWS))
    column = jnp.sum(jnp.where(first == second, spread, 0.0), axis=1, keepdims=True)
    before = (column == spread) & (first < second)
    rank = jnp.sum(jnp.where(before, 1.0, 0.0), axis=0, keepdims=True)
    slot = rank - (round_index * SLOTS).astype(F32)
    hot = iota((SLOTS, ROWS), 0).astype(F32) == slot
    return column, jnp.where(hot, 1.0, 0.0)


def pack_kernel(round_ref, virt_s, virt_v, pairs_v, amp_ref, out_ref, kept, wide):
    row = local_labels(pairs_v)
    column, hot = slots_of(row, round_ref[0])
    hot = hot.astype(BF16)
    column = column.astype(I32)
    base = lax.axis_index("virt") * OWN_C
    labels = virt_v[...].reshape(1, WIDTH)
    wide[:, :, 384:DEPTH_PAD] = jnp.zeros((OWNERS, SLOTS, DEPTH_PAD - 384), F32)
    for c in range(OWN_C):
        key = jnp.bitwise_xor(labels, virt_s[base + c])
        start = c * WIDTH_PAD
        kept[:, start : start + WIDTH] = jnp.where(column == key, amp_ref[c].astype(F32), 0.0).astype(BF16)
    packed = jnp.dot(hot, kept[...], preferred_element_type=F32)
    for c in range(OWN_C):
        for owner in range(OWNERS):
            start = c * WIDTH_PAD + owner * OWN_D
            wide[owner, :, c * OWN_D : (c + 1) * OWN_D] = packed[:, start : start + OWN_D]
    out_ref[...] = wide[...].astype(BF16)


def tile_column(tile_s):
    column = jnp.zeros((TILE, 1), I32)
    place = iota((TILE, 1), 0)
    for b in range(TILE):
        column = jnp.where(place == b, tile_s[b], column)
    return column


def mask_kernel(
    round_ref, virt_s, tile_s, virt_v, int_hbm, near_ref, far_hbm, slabs, masks, turn, wide, far, sems, far_sems
):
    del round_ref

    def load(c):
        return pltpu.make_async_copy(int_hbm.at[c], slabs.at[c], sems.at[c])

    def save(step):
        rows = pl.ds(pl.multiple_of(step * 2 * OWN_D, 16), 2 * OWN_D)
        return pltpu.make_async_copy(far.at[:, rows, :], far_hbm.at[:, rows, :], far_sems.at[step])

    for c in range(OWN_C):
        load(c).start()
    label = jnp.bitwise_xor(tile_column(tile_s), virt_v[...].reshape(1, WIDTH))
    for g in range(8):
        masks[g] = jnp.where(label == g, 1.0, 0.0).astype(BF16)
    high, low = iota((256, 256), 0), iota((256, 256), 1)
    match = (high // 16 == low % 16) & (high % 16 == low // 16)
    turn[...] = jnp.where(match, 1.0, 0.0).astype(BF16)
    base_c = lax.axis_index("virt") * OWN_C
    base_d = lax.axis_index("pair") * OWN_D

    @pl.loop(0, OWN_C // 2)
    def _(step):
        load(step * 2).wait()
        load(step * 2 + 1).wait()
        for group in range(GROUPS):
            for k in range(16):
                c, d = divmod(group * 16 + k, OWN_D)
                g = jnp.bitwise_xor(virt_s[base_c + step * 2 + c], virt_s[base_d + d])
                start = group * WIDTH_PAD
                wide[k * 16 : (k + 1) * 16, start : start + WIDTH] = slabs[step * 2 + c, d] * masks[g]
        turned = jnp.dot(turn[...], wide[...], preferred_element_type=F32).astype(BF16)
        for group in range(GROUPS):
            start = group * WIDTH_PAD
            rows = pl.ds(pl.multiple_of(step * 2 * OWN_D + group * 16, 16), 16)
            for b in range(TILE):
                pair, side = divmod(b, 2)
                out, at = (near_ref, pair) if pair < NEAR else (far, pair - NEAR)
                out[at, rows, side * WIDTH : (side + 1) * WIDTH] = turned[
                    b * 16 : (b + 1) * 16, start : start + WIDTH
                ]
        save(step).start()

    @pl.loop(0, OWN_C // 2)
    def _(step):
        save(step).wait()


def products(core, amp_ref, near_ref, far_hbm, left, far, sem, put):
    load = pltpu.make_async_copy(far_hbm, far, sem)
    load.start()
    x = lax.axis_index("pair") // CORES
    for at, hop in enumerate(HOPS):
        owner = lax.rem(x + hop, CHIPS) * CORES + core
        left[at * SLOTS : (at + 1) * SLOTS, :] = amp_ref[owner].astype(F32)
    rows = left[...].astype(BF16)[:, :DEPTH]
    for pair in range(NEAR):
        put(pair, jnp.dot(rows, near_ref[pair], preferred_element_type=F32))
    load.wait()
    for pair in range(FAR):
        put(NEAR + pair, jnp.dot(rows, far[pair], preferred_element_type=F32))


def scale_code(largest):
    return jnp.ceil(FINE * jnp.log2(jnp.maximum(largest, 1e-36))).astype(I32)


def scale_up(code):
    return FULL * jnp.exp2(code.astype(F32) * (-1.0 / FINE))


def scale_down(code):
    return jnp.exp2(code.astype(F32) * (1.0 / FINE)) * (1.0 / FULL)


def joined(high, low, factor):
    high = jnp.round(high * factor).astype(I32)
    low = jnp.round(low * factor).astype(I32)
    return jnp.left_shift(high, 16) | (low & 0xFFFF)


def high_of(word):
    return jnp.right_shift(word, 16).astype(F32)


def low_of(word):
    return jnp.right_shift(jnp.left_shift(word, 16), 16).astype(F32)


def row_largest(values):
    top = jnp.abs(values[0])
    for pair in range(1, PAIRS_B):
        top = jnp.maximum(top, jnp.abs(values[pair]))
    return jnp.max(top, axis=1, keepdims=True)


def write_words(values, outs):
    code = scale_code(row_largest(values))
    factor = scale_up(code)
    tail = jnp.broadcast_to(code, (code.shape[0], MESSAGE - WORDS))
    for pair in range(PAIRS_B // 2):
        words = joined(values[pair], values[pair + PAIRS_B // 2], factor)
        start = 0
        for out in outs:
            stop = start + out.shape[0]
            out[:, pair * PAIR : (pair + 1) * PAIR] = words[start:stop]
            start = stop
    start = 0
    for out in outs:
        stop = start + out.shape[0]
        out[:, WORDS:MESSAGE] = tail[start:stop]
        start = stop


def send_kernel(amp_ref, near_ref, far_hbm, far_out, rest_out, left, far, sem, values):
    def put(pair, value):
        values[pair] = value

    products(1 - lax.axis_index("pair") % CORES, amp_ref, near_ref, far_hbm, left, far, sem, put)
    write_words(values, (far_out, rest_out))


def keep_kernel(amp_ref, near_ref, far_hbm, far_out, rest_out, left, far, sem):
    def put(pair, value):
        far_out[pair] = value[0:SLOTS]
        rest_out[pair] = value[SLOTS:CORE_ROWS]

    products(lax.axis_index("pair") % CORES, amp_ref, near_ref, far_hbm, left, far, sem, put)


def add_words(words, values, start):
    factor = scale_down(words[:, WORDS : WORDS + 1])
    for pair in range(PAIRS_B // 2):
        word = words[:, pair * PAIR : (pair + 1) * PAIR]
        other = pair + PAIRS_B // 2
        values[pair] = start[pair] + high_of(word) * factor
        values[other] = start[other] + low_of(word) * factor


def two_kernel(keep_ref, got_ref, two_ref, values):
    add_words(got_ref, values, keep_ref)
    write_words(values, (two_ref,))


def near_kernel(keep_ref, got_ref, one_ref, three_ref, own_ref, values):
    add_words(got_ref, values, keep_ref)
    for pair in range(PAIRS_B):
        own_ref[pair] = values[pair, 2 * SLOTS : REST, :]
    write_words(values.at[:, 0 : 2 * SLOTS, :], (one_ref, three_ref))


def piece(group, b):
    index = group * HALF + b
    return 8 * (index // 12), OWN_A * (index % 12)


def column_kernel(own_ref, one_ref, two_ref, three_ref, out_ref, values, words):
    add_words(one_ref, values, own_ref)
    add_words(two_ref, values, values)
    add_words(three_ref, values, values)
    write_words(values, (words,))
    code = words[:, WORDS : WORDS + 8]
    lane = iota((8, 8), 1)
    tail = jnp.where(lane == 0, code[0:8], jnp.where(lane == 1, code[8:16], code[16:24]))
    for j in range(COLUMNS):
        for group in range(SLOTS // 8):
            for b in range(HALF):
                row, lane_at = piece(group, b)
                start = b * WIDTH + j * OWN_A
                out_ref[j, row : row + 8, lane_at : lane_at + OWN_A] = words[
                    group * 8 : group * 8 + 8, start : start + OWN_A
                ]
        out_ref[j, 0:8, 120:128] = tail
        out_ref[j, 8:16, 120:128] = tail


def final_kernel(round_ref, virt_s, tile_s, pairs_v, got_ref, out_ref, flat):
    row = local_labels(pairs_v)
    _, hot = slots_of(row, round_ref[0])
    lane = iota((8, 128), 1)
    sums = [[jnp.zeros((8, 128), F32) for _ in range(2)] for _ in range(2)]
    for j in range(COLUMNS):
        for block in range(2):
            word = got_ref[j, 8 * block : 8 * block + 8, :]
            if block == 0:
                code = jnp.where(lane < 80, word[:, 120:121], word[:, 121:122])
            else:
                code = jnp.where(lane < 40, word[:, 121:122], word[:, 122:123])
            factor = scale_down(code)
            sums[0][block] += high_of(word) * factor
            sums[1][block] += low_of(word) * factor
    for half in range(2):
        for group in range(SLOTS // 8):
            for b in range(HALF):
                at, lane_at = piece(group, b)
                to = (half * HALF + b) * OWN_A
                flat[group * 8 : group * 8 + 8, to : to + OWN_A] = sums[half][at // 8][:, lane_at : lane_at + OWN_A]
    spread = lax.dot_general(
        flat[...], hot, (((0,), (0,)), ((), ())), precision=lax.Precision.HIGHEST, preferred_element_type=F32
    )
    base = lax.axis_index("virt") * OWN_A
    column = tile_column(tile_s)
    for a in range(OWN_A):
        for b in range(TILE):
            out_ref[a, b : b + 1, :] = spread[b * OWN_A + a : b * OWN_A + a + 1]
        keep = jnp.bitwise_xor(column, virt_s[base + a]) == row
        out_ref[a] = jnp.where(keep, out_ref[a], 0.0)


def shape(dims, dtype):
    return jax.ShapeDtypeStruct(dims, dtype)


def masked_integrals(number, integrals, virt, tile):
    return pl.pallas_call(
        mask_kernel,
        out_shape=[pltpu.VMEM((NEAR, DEPTH, PAIR), BF16), pltpu.HBM((FAR, DEPTH, PAIR), BF16)],
        in_specs=[SMEM, SMEM, SMEM, VMEM, HBM],
        out_specs=[VMEM, HBM],
        scratch_shapes=[
            pltpu.VMEM((OWN_C, OWN_D, TILE, WIDTH), BF16),
            pltpu.VMEM((8, TILE, WIDTH), BF16),
            pltpu.VMEM((256, 256), BF16),
            pltpu.VMEM((256, GROUPS * WIDTH_PAD), BF16),
            pltpu.VMEM((FAR, DEPTH, PAIR), BF16),
            pltpu.SemaphoreType.DMA((OWN_C,)),
            pltpu.SemaphoreType.DMA((OWN_C // 2,)),
        ],
        compiler_params=params(),
        name="mask_turn",
        cost_estimate=pl.CostEstimate(flops=1 << 30, bytes_accessed=10 << 20, transcendentals=0),
    )(number, virt, tile, virt, pltpu.with_memory_space_constraint(integrals, pltpu.HBM))


def one_round(round_index, amplitudes, integrals, virt, tile, pairs):
    number = jnp.reshape(round_index, (1,)).astype(I32)
    packed = pl.pallas_call(
        pack_kernel,
        out_shape=shape((OWNERS, SLOTS, DEPTH_PAD), BF16),
        in_specs=[SMEM, SMEM, VMEM, VMEM, VMEM],
        out_specs=VMEM,
        scratch_shapes=[
            pltpu.VMEM((ROWS, OWN_C * WIDTH_PAD), BF16),
            pltpu.VMEM((OWNERS, SLOTS, DEPTH_PAD), F32),
        ],
        compiler_params=params(),
        name="pack",
    )(number, virt, virt, pairs, pltpu.with_memory_space_constraint(jnp.transpose(amplitudes, (1, 0, 2)), pltpu.HBM))
    amp = lax.all_to_all(packed, "pair", split_axis=0, concat_axis=0, tiled=True)
    near, far = masked_integrals(number, integrals, virt, tile)
    far = pltpu.with_memory_space_constraint(far, pltpu.HBM)
    left = pltpu.VMEM((CORE_ROWS, DEPTH_PAD), F32)
    table = pltpu.VMEM((PAIRS_B, CORE_ROWS, PAIR), F32)
    work = [left, pltpu.VMEM((FAR, DEPTH, PAIR), BF16), pltpu.SemaphoreType.DMA]
    message = shape((SLOTS, MESSAGE), I32)
    send = pl.pallas_call(
        send_kernel,
        out_shape=[message, shape((REST, MESSAGE), I32)],
        in_specs=[VMEM, VMEM, HBM],
        out_specs=[VMEM] * 2,
        scratch_shapes=[*work, table],
        compiler_params=params(),
        name="send_rows",
    )(amp, near, far)
    got = [lax.ppermute(part, "pair", [(i, i ^ 1) for i in range(OWNERS)]) for part in send]
    keep = pl.pallas_call(
        keep_kernel,
        out_shape=[shape((PAIRS_B, SLOTS, PAIR), F32), shape((PAIRS_B, REST, PAIR), F32)],
        in_specs=[VMEM, VMEM, HBM],
        out_specs=[VMEM] * 2,
        scratch_shapes=work,
        compiler_params=params(),
        name="keep_rows",
        cost_estimate=pl.CostEstimate(flops=1 << 29, bytes_accessed=8 << 20, transcendentals=0),
    )(amp, near, far)
    two = pl.pallas_call(
        two_kernel,
        out_shape=message,
        in_specs=[VMEM] * 2,
        out_specs=VMEM,
        scratch_shapes=[pltpu.VMEM((PAIRS_B, SLOTS, PAIR), F32)],
        compiler_params=params(),
        name="chip_sum_two",
    )(keep[0], got[0])
    one, three, own = pl.pallas_call(
        near_kernel,
        out_shape=[message, message, shape((PAIRS_B, SLOTS, PAIR), F32)],
        in_specs=[VMEM] * 2,
        out_specs=[VMEM] * 3,
        scratch_shapes=[pltpu.VMEM((PAIRS_B, REST, PAIR), F32)],
        compiler_params=params(),
        name="chip_sum_near",
    )(keep[1], got[1])
    hops = [
        lax.ppermute(part, "pair", [(i, (i + CORES * hop) % OWNERS) for i in range(OWNERS)])
        for hop, part in ((2, two), (1, one), (3, three))
    ]
    parts = pl.pallas_call(
        column_kernel,
        out_shape=shape((COLUMNS, 16, 128), I32),
        in_specs=[VMEM] * 4,
        out_specs=VMEM,
        scratch_shapes=[pltpu.VMEM((PAIRS_B, SLOTS, PAIR), F32), pltpu.VMEM((SLOTS, MESSAGE), I32)],
        compiler_params=params(),
        name="column_sum",
    )(own, *hops)
    back = lax.all_to_all(parts, "virt", split_axis=0, concat_axis=0, tiled=True)
    return pl.pallas_call(
        final_kernel,
        out_shape=pltpu.HBM((OWN_A, TILE, ROWS), F32),
        in_specs=[SMEM, SMEM, SMEM, VMEM, VMEM],
        out_specs=VMEM,
        scratch_shapes=[pltpu.VMEM((SLOTS, TILE * OWN_A), F32)],
        compiler_params=params(),
        name="unpack",
    )(number, virt, tile, pairs, back)


def body(amplitudes, integrals, virt_irrep, tile_irrep, pair_irrep):
    run = functools.partial(
        one_round,
        amplitudes=amplitudes,
        integrals=integrals,
        virt=virt_irrep,
        tile=tile_irrep,
        pairs=pair_irrep,
    )
    counts = jnp.sum(
        (pair_irrep.reshape(OWNERS, ROWS)[:, :, None] == jnp.arange(8)).astype(I32), axis=1
    )
    rounds = (jnp.max(counts) + SLOTS - 1) // SLOTS
    first = run(jnp.zeros((), I32))
    _, total = lax.while_loop(
        lambda state: state[0] < rounds,
        lambda state: (state[0] + 1, state[1] + run(state[0])),
        (jnp.ones((), I32), first),
    )
    return jnp.transpose(total, (2, 1, 0))


def solution(mesh):
    in_specs = (P("pair", "virt", None), P("virt", "pair", None, None), P(), P(), P())
    out_specs = P("pair", None, "virt")
    return jax.shard_map(body, mesh=mesh, in_specs=in_specs, out_specs=out_specs, check_vma=False)
```

time: 69.6 us -> 62.7 us (0.901)
  local copies, waits for them, and re-layouts: 4.5 us -> 0.09 us
  waiting for transfers between devices: 24.8 us -> 22.7 us
  Pallas kernels: 18.5 us -> 17 us
  starting transfers between devices: 19.5 us -> 20.5 us
    unnamed x14 -> x6, local copies, waits for them, and re-layouts: 3.05 us -> 0.02 us
    reshape x4 -> x0, local copies, waits for them, and re-layouts: 1.38 us -> none  [the longest x2 0.69 us: one_round(): pair_row = pairs.reshape(1, OWNERS * ROWS)]
    ppermute x3, waiting for transfers between devices: 12.5 us -> 11.3 us  [one_round(): lax.ppermute(part, 'pair', [(i, (i + CORES * hop) % OWNERS) for i in rang...]
    ppermute x1 -> x2, waiting for transfers between devices: 1.43 us -> 0.49 us  [one_round(): lax.ppermute(part, 'pair', [(i, i ^ 1) for i in range(OWNERS)])]
    pallas_call x5 -> x6, Pallas kernels: 13.2 us -> 12.4 us  [the longest x1 5.73 us: masked_integrals(): pl.pallas_call(mask_kernel, out_shape=[pltpu.VMEM((NEAR, DEPTH, PAIR), BF...]
  transfers between devices with their start and end apart: 6 -> 7, of which waited for: 5 -> 5; matrix products, arithmetic and copies ran while one was open for 1% -> 1% of each run, Pallas kernels for 9% -> 13%
where the time goes in v2:
time: 62.7 us; the launch traced here: 61.9 us
  waiting for transfers between devices  22.7 us (36%)
  starting transfers between devices  20.5 us (33%)
  Pallas kernels  17 us (27%)
  other arithmetic  0.85 us (1%)
  between operations  0.77 us (1%)
    ppermute x3, waiting for transfers between devices, one_round(): lax.ppermute(part, 'pair', [(i, (i + CORES * hop) % OWNERS) for i in rang...  11.3 us
    all_to_all x1, waiting for transfers between devices, one_round(): lax.all_to_all(parts, 'virt', split_axis=0, concat_axis=0, tiled=True)  10.9 us
    all_to_all x1, starting transfers between devices, one_round(): lax.all_to_all(parts, 'virt', split_axis=0, concat_axis=0, tiled=True)  10.7 us
    pallas_call x1, Pallas kernels, masked_integrals(): pl.pallas_call(mask_kernel, out_shape=[pltpu.VMEM((NEAR, DEPTH, PAIR), BF...  5.73 us
    all_to_all x1, starting transfers between devices, one_round(): lax.all_to_all(packed, 'pair', split_axis=0, concat_axis=0, tiled=True)  5.54 us
    ppermute x3, starting transfers between devices, one_round(): lax.ppermute(part, 'pair', [(i, (i + CORES * hop) % OWNERS) for i in rang...  3.66 us
    pallas_call x1, Pallas kernels, one_round(): pl.pallas_call(pack_kernel, out_shape=shape((OWNERS, SLOTS, DEPTH_PAD), B...  2.59 us
    pallas_call x1, Pallas kernels, one_round(): pl.pallas_call(send_kernel, out_shape=[message, shape((REST, MESSAGE), I3...  2.42 us
  transfers between devices with their start and end apart: 7, of which 5 were waited for; matrix products, arithmetic and copies ran while one was open for 1% of the time, Pallas kernels for 13%

profile of v2, /device:TPU:6, one launch (start us, length us, event | category | flops | bytes accessed | tf_op | source)
XLA Modules:
  0.0 61.9 jit_solution(18056410455220207726)
XLA Ops:
  0.0 2.6 %pack.2 = bf16[8,24,512]{2,1,0:T(8,128)(2,1)} custom-call(s32[1]{0:T(128)} %constant.16.clone.1.round_ref, s32[320]{0:T(512)} %virt_s.5, s32[320]{0:T(512)} %virt_s.5, s32[640]{0:T(1024)} %pairs_v.3, bf16[10,80,320]{2,1,0:T(8,128)(2,1)} %bitcast.8), custom_call_target="tpu_custom_call" | custom-call | tf_op jit(solution)/shard_map/pack/pallas_call | solution.py:339
  2.6 5.5 %all-to-all-start.2 = ((bf16[8,24,512]{2,1,0:T(8,128)(2,1)}), bf16[8,24,512]{2,1,0:T(8,128)(2,1)S(1)}, u32[]{:S(2)}, u32[]{:S(2)}) async-start(bf16[8,24,512]{2,1,0:T(8,128)(2,1)} %pack.2), calls=%async_computation.2 | async-start | bytes 393216 | tf_op jit(solution)/shard_map/all_to_all | solution.py:351
  8.1 5.7 %mask_turn.2 = (bf16[6,400,640]{2,1,0:T(8,128)(2,1)S(1)}, bf16[2,400,640]{2,1,0:T(8,128)(2,1)}) custom-call(s32[1]{0:T(128)} %constant.16.clone.1.round_ref, s32[320]{0:T(512)} %virt_s.5, s32[16]{0:T(128)} %tile_s.3, s32[320]{0:T(512)} %virt_s.5, bf16[10,40,16,320]{3,2,1,0:T(8,128)(2,1)} %int_hbm.1), custom_call_target="tpu_custom_call" | custom-call | flops 1073741824 | bytes 10485760 | tf_op jit(solution)/shard_map/mask_turn/pallas_call | solution.py:317
  13.9 0.0 all-to-all-done.2.amp_ref
  13.9 2.4 %send_rows.2 = (s32[24,2688]{1,0:T(8,128)S(1)}, s32[72,2688]{1,0:T(8,128)S(1)}) custom-call(bf16[8,24,512]{2,1,0:T(8,128)(2,1)S(1)} %all-to-all-done.2.amp_ref, bf16[6,400,640]{2,1,0:T(8,128)(2,1)S(1)} %get-tuple-element.66.near_ref, bf16[2,400,640]{2,1,0:T(8,128)(2,1)} %get-tuple-element.67.far_hbm), custom_call_target="tpu_custom_call" | custom-call | tf_op jit(solution)/shard_map/send_rows/pallas_call | solution.py:358
  16.3 0.2 collective-permute-start.5
  16.5 0.4 collective-permute-start.6
  16.9 1.6 %keep_rows.2 = (f32[8,24,640]{2,1,0:T(8,128)S(1)}, f32[8,72,640]{2,1,0:T(8,128)S(1)}) custom-call(bf16[8,24,512]{2,1,0:T(8,128)(2,1)S(1)} %all-to-all-done.2.amp_ref, bf16[6,400,640]{2,1,0:T(8,128)(2,1)S(1)} %get-tuple-element.66.near_ref, bf16[2,400,640]{2,1,0:T(8,128)(2,1)} %get-tuple-element.67.far_hbm), custom_call_target="tpu_custom_call" | custom-call | flops 536870912 | bytes 8388608 | tf_op jit(solution)/shard_map/keep_rows/pallas_call | solution.py:368
  18.5 0.0 copy-start.3
  18.5 0.0 copy-start.2
  18.5 0.0 copy-start.4
  18.5 0.5 collective-permute-done.6.got_ref
  19.0 0.3 chip_sum_two.2
  19.3 1.5 %collective-permute-start.7 = (s32[24,2688]{1,0:T(8,128)S(1)}, s32[24,2688]{1,0:T(8,128)S(1)}, u32[]{:S(2)}, u32[]{:S(2)}) collective-permute-start(s32[24,2688]{1,0:T(8,128)S(1)} %chip_sum_two.2), channel_id=1, source_target_pairs={{0,128},{32,160},{64,192},{96,224},{128,0},{160,32},{192,64},{224,... | collective-permute-start | bytes 774152 | tf_op jit(solution)/shard_map/ppermute | solution.py:397
  20.8 0.0 collective-permute-done.5.got_ref
  20.8 0.5 chip_sum_near.2
  21.3 2.1 %collective-permute-start.8 = (s32[24,2688]{1,0:T(8,128)S(1)}, s32[24,2688]{1,0:T(8,128)S(1)}, u32[]{:S(2)}, u32[]{:S(2)}) collective-permute-start(s32[24,2688]{1,0:T(8,128)S(1)} %get-tuple-element.73), channel_id=1, source_target_pairs={{0,64},{32,96},{64,128},{96,160},{128,192},{160,224},{192,0},{224,... | collective-permute-start | bytes 774152 | tf_op jit(solution)/shard_map/ppermute | solution.py:397
  23.4 0.0 collective-permute-start.9
  23.4 6.5 %collective-permute-done.7.one_ref = s32[24,2688]{1,0:T(8,128)S(1)} collective-permute-done((s32[24,2688]{1,0:T(8,128)S(1)}, s32[24,2688]{1,0:T(8,128)S(1)}, u32[]{:S(2)}, u32[]{:S(2)}) %collective-permute-start.7) | collective-permute-done | bytes 258080 | tf_op jit(solution)/shard_map/ppermute | solution.py:397
  30.0 3.2 %collective-permute-done.8.two_ref = s32[24,2688]{1,0:T(8,128)S(1)} collective-permute-done((s32[24,2688]{1,0:T(8,128)S(1)}, s32[24,2688]{1,0:T(8,128)S(1)}, u32[]{:S(2)}, u32[]{:S(2)}) %collective-permute-start.8) | collective-permute-done | bytes 258080 | tf_op jit(solution)/shard_map/ppermute | solution.py:397
  33.2 1.5 %collective-permute-done.9.three_ref = s32[24,2688]{1,0:T(8,128)S(1)} collective-permute-done((s32[24,2688]{1,0:T(8,128)S(1)}, s32[24,2688]{1,0:T(8,128)S(1)}, u32[]{:S(2)}, u32[]{:S(2)}) %collective-permute-start.9) | collective-permute-done | bytes 258080 | tf_op jit(solution)/shard_map/ppermute | solution.py:397
  34.7 2.0 %column_sum.2 = s32[32,16,128]{2,1,0:T(8,128)} custom-call(f32[8,24,640]{2,1,0:T(8,128)S(1)} %get-tuple-element.70.own_ref, s32[24,2688]{1,0:T(8,128)S(1)} %collective-permute-done.7.one_ref, s32[24,2688]{1,0:T(8,128)S(1)} %collective-permute-done.8.two_ref, s32[24,2688]{1,0:T(8,128)S(1)} %collective-permute-done.9.three_ref), custom_call_target="tpu_custom_call" | custom-call | tf_op jit(solution)/shard_map/column_sum/pallas_call | solution.py:400
  36.7 10.7 %all-to-all-start.3 = ((s32[32,16,128]{2,1,0:T(8,128)}), s32[32,16,128]{2,1,0:T(8,128)S(1)}, u32[]{:S(2)}, u32[]{:S(2)}) async-start(s32[32,16,128]{2,1,0:T(8,128)} %column_sum.2), calls=%async_computation.3 | async-start | bytes 524288 | tf_op jit(solution)/shard_map/all_to_all | solution.py:409
  47.4 0.0 copy-done.3
  47.4 0.1 eq.15
  47.5 0.2 convert_reduce_fusion
  47.7 0.6 %reduce_max.9 = s32[]{:T(128)} reduce(s32[8,8]{1,0:T(8,128)S(1)} %convert_reduce_fusion, s32[]{:T(128)} %constant.18.clone.1), dimensions={0,1}, to_apply=%region_1.0 | reduce | flops 63 | bytes 264 | tf_op jit(solution)/shard_map/reduce_max | solution.py:433
  49.1 10.9 %all-to-all-done.3.got_ref = s32[32,16,128]{2,1,0:T(8,128)S(1)} async-done(((s32[32,16,128]{2,1,0:T(8,128)}), s32[32,16,128]{2,1,0:T(8,128)S(1)}, u32[]{:S(2)}, u32[]{:S(2)}) %all-to-all-start.3) | async-done | bytes 262176 | tf_op jit(solution)/shard_map/all_to_all | solution.py:409
  60.0 0.0 copy-done.2
  60.0 0.0 copy-done.4
  60.0 1.9 %unpack.2 = f32[10,16,80]{2,1,0:T(8,128)} custom-call(s32[1]{0:T(128)} %constant.16.clone.1.round_ref, s32[320]{0:T(512)S(1)} %copy-done.2, s32[16]{0:T(128)S(1)} %copy-done.4, s32[640]{0:T(1024)S(1)} %copy-done.3, s32[32,16,128]{2,1,0:T(8,128)S(1)} %all-to-all-done.3.got_ref), custom_call_target="tpu_custom_call" | custom-call | tf_op jit(solution)/shard_map/unpack/pallas_call | solution.py:410
  (1 shorter events, 0.0 us)
Async XLA Ops:
  2.6 11.3 %all-to-all-start.2 = ((bf16[8,24,512]{2,1,0:T(8,128)(2,1)}), bf16[8,24,512]{2,1,0:T(8,128)(2,1)S(1)}, u32[]{:S(2)}, u32[]{:S(2)}) async-start(bf16[8,24,512]{2,1,0:T(8,128)(2,1)} %pack.2), calls=%async_computation.2 | async-start | bytes 393216 | tf_op jit(solution)/shard_map/all_to_all | solution.py:351
  16.3 4.5 %collective-permute-start.5 = (s32[72,2688]{1,0:T(8,128)S(1)}, s32[72,2688]{1,0:T(8,128)S(1)}, u32[]{:S(2)}, u32[]{:S(2)}) collective-permute-start(s32[72,2688]{1,0:T(8,128)S(1)} %get-tuple-element.69), channel_id=1, source_target_pairs={{0,32},{32,0},{64,96},{96,64},{128,160},{160,128},{192,224},{224,1... | collective-permute-start | bytes 2322440 | tf_op jit(solution)/shard_map/ppermute | solution.py:367
  16.5 2.5 %collective-permute-start.6 = (s32[24,2688]{1,0:T(8,128)S(1)}, s32[24,2688]{1,0:T(8,128)S(1)}, u32[]{:S(2)}, u32[]{:S(2)}) collective-permute-start(s32[24,2688]{1,0:T(8,128)S(1)} %get-tuple-element.72), channel_id=1, source_target_pairs={{0,32},{32,0},{64,96},{96,64},{128,160},{160,128},{192,224},{224,1... | collective-permute-start | bytes 774152 | tf_op jit(solution)/shard_map/ppermute | solution.py:367
  18.5 28.9 %copy-start.3 = (s32[640]{0:T(1024)S(1)}, s32[640]{0:T(1024)}, u32[]{:S(2)}) copy-start(s32[640]{0:T(1024)} %pairs_v.3) | copy-start | bytes 7684
  18.5 41.5 %copy-start.2 = (s32[320]{0:T(512)S(1)}, s32[320]{0:T(512)}, u32[]{:S(2)}) copy-start(s32[320]{0:T(512)} %virt_s.5) | copy-start | bytes 3844
  18.5 41.5 %copy-start.4 = (s32[16]{0:T(128)S(1)}, s32[16]{0:T(128)}, u32[]{:S(2)}) copy-start(s32[16]{0:T(128)} %tile_s.3) | copy-start | bytes 196
  19.3 10.7 %collective-permute-start.7 = (s32[24,2688]{1,0:T(8,128)S(1)}, s32[24,2688]{1,0:T(8,128)S(1)}, u32[]{:S(2)}, u32[]{:S(2)}) collective-permute-start(s32[24,2688]{1,0:T(8,128)S(1)} %chip_sum_two.2), channel_id=1, source_target_pairs={{0,128},{32,160},{64,192},{96,224},{128,0},{160,32},{192,64},{224,... | collective-permute-start | bytes 774152 | tf_op jit(solution)/shard_map/ppermute | solution.py:397
  21.3 11.9 %collective-permute-start.8 = (s32[24,2688]{1,0:T(8,128)S(1)}, s32[24,2688]{1,0:T(8,128)S(1)}, u32[]{:S(2)}, u32[]{:S(2)}) collective-permute-start(s32[24,2688]{1,0:T(8,128)S(1)} %get-tuple-element.73), channel_id=1, source_target_pairs={{0,64},{32,96},{64,128},{96,160},{128,192},{160,224},{192,0},{224,... | collective-permute-start | bytes 774152 | tf_op jit(solution)/shard_map/ppermute | solution.py:397
  23.4 11.3 %collective-permute-start.9 = (s32[24,2688]{1,0:T(8,128)S(1)}, s32[24,2688]{1,0:T(8,128)S(1)}, u32[]{:S(2)}, u32[]{:S(2)}) collective-permute-start(s32[24,2688]{1,0:T(8,128)S(1)} %get-tuple-element.74), channel_id=1, source_target_pairs={{0,192},{32,224},{64,0},{96,32},{128,64},{160,96},{192,128},{224,1... | collective-permute-start | bytes 774152 | tf_op jit(solution)/shard_map/ppermute | solution.py:397
  36.7 23.3 %all-to-all-start.3 = ((s32[32,16,128]{2,1,0:T(8,128)}), s32[32,16,128]{2,1,0:T(8,128)S(1)}, u32[]{:S(2)}, u32[]{:S(2)}) async-start(s32[32,16,128]{2,1,0:T(8,128)} %column_sum.2), calls=%async_computation.3 | async-start | bytes 524288 | tf_op jit(solution)/shard_map/all_to_all | solution.py:409

commit v3 on v2

--- a/solution.py
+++ b/solution.py
@@ -27,8 +27,9 @@
 WORDS = HALF * WIDTH
 MESSAGE = WORDS + 128
 CORE_ROWS = CHIPS * SLOTS
-HOPS = (2, 1, 3, 0)
-REST = CORE_ROWS - SLOTS
+LAYERS = 8
+TILES = WORDS // 128
+BLOCK = (TILES + 1) * SLOTS
 FINE = 64.0
 FULL = 32767.0
 WIDTH_PAD = 384
@@ -152,8 +153,8 @@
     load = pltpu.make_async_copy(far_hbm, far, sem)
     load.start()
     x = lax.axis_index("pair") // CORES
-    for at, hop in enumerate(HOPS):
-        owner = lax.rem(x + hop, CHIPS) * CORES + core
+    for at in range(CHIPS):
+        owner = jnp.where(core == 0, lax.rem(x + at, CHIPS), at) * CORES + core
         left[at * SLOTS : (at + 1) * SLOTS, :] = amp_ref[owner].astype(F32)
     rows = left[...].astype(BF16)[:, :DEPTH]
     for pair in range(NEAR):
@@ -196,36 +197,25 @@
     return jnp.max(top, axis=1, keepdims=True)
 
 
-def write_words(values, outs):
+def write_words(values, out_ref):
     code = scale_code(row_largest(values))
     factor = scale_up(code)
-    tail = jnp.broadcast_to(code, (code.shape[0], MESSAGE - WORDS))
     for pair in range(PAIRS_B // 2):
-        words = joined(values[pair], values[pair + PAIRS_B // 2], factor)
-        start = 0
-        for out in outs:
-            stop = start + out.shape[0]
-            out[:, pair * PAIR : (pair + 1) * PAIR] = words[start:stop]
-            start = stop
-    start = 0
-    for out in outs:
-        stop = start + out.shape[0]
-        out[:, WORDS:MESSAGE] = tail[start:stop]
-        start = stop
-
-
-def send_kernel(amp_ref, near_ref, far_hbm, far_out, rest_out, left, far, sem, values):
+        out_ref[:, pair * PAIR : (pair + 1) * PAIR] = joined(values[pair], values[pair + PAIRS_B // 2], factor)
+    out_ref[:, WORDS:MESSAGE] = jnp.broadcast_to(code, (code.shape[0], MESSAGE - WORDS))
+
+
+def send_kernel(amp_ref, near_ref, far_hbm, out_ref, left, far, sem, values):
     def put(pair, value):
         values[pair] = value
 
     products(1 - lax.axis_index("pair") % CORES, amp_ref, near_ref, far_hbm, left, far, sem, put)
-    write_words(values, (far_out, rest_out))
-
-
-def keep_kernel(amp_ref, near_ref, far_hbm, far_out, rest_out, left, far, sem):
+    write_words(values, out_ref)
+
+
+def keep_kernel(amp_ref, near_ref, far_hbm, out_ref, left, far, sem):
     def put(pair, value):
-        far_out[pair] = value[0:SLOTS]
-        rest_out[pair] = value[SLOTS:CORE_ROWS]
+        out_ref[pair] = value
 
     products(lax.axis_index("pair") % CORES, amp_ref, near_ref, far_hbm, left, far, sem, put)
 
@@ -239,16 +229,47 @@
         values[other] = start[other] + low_of(word) * factor
 
 
-def two_kernel(keep_ref, got_ref, two_ref, values):
+def crossing(start, length):
+    cuts, at = [], 0
+    while at < length:
+        tile, lane = divmod(start + at, 128)
+        size = min(length - at, 128 - lane)
+        cuts.append((at, tile, lane, size))
+        at += size
+    return cuts
+
+
+def chip_kernel(keep_ref, got_ref, own_ref, one_ref, two_ref, three_ref, values, words, spread):
+    core = lax.axis_index("pair") % CORES
+    outs = (own_ref, one_ref, two_ref, three_ref)
     add_words(got_ref, values, keep_ref)
-    write_words(values, (two_ref,))
-
-
-def near_kernel(keep_ref, got_ref, one_ref, three_ref, own_ref, values):
-    add_words(got_ref, values, keep_ref)
-    for pair in range(PAIRS_B):
-        own_ref[pair] = values[pair, 2 * SLOTS : REST, :]
-    write_words(values.at[:, 0 : 2 * SLOTS, :], (one_ref, three_ref))
+    write_words(values, words)
+
+    @pl.when(core == 0)
+    def _():
+        for hop, out in enumerate(outs):
+            for tile in range(TILES + 1):
+                out[tile * SLOTS : (tile + 1) * SLOTS, :] = words[
+                    hop * SLOTS : (hop + 1) * SLOTS, tile * 128 : (tile + 1) * 128
+                ]
+
+    @pl.when(core == 1)
+    def _():
+        own_width = WIDTH // CHIPS
+        lane = iota((SLOTS, 128), 1)
+        codes = [words[q * SLOTS : (q + 1) * SLOTS, WORDS:MESSAGE] for q in range(CHIPS)]
+        tail = jnp.where(lane == 0, codes[0], jnp.where(lane == 1, codes[1], jnp.where(lane == 2, codes[2], codes[3])))
+        for y in range(CHIPS):
+            for b in range(HALF):
+                for at, tile, to, size in crossing(b * own_width, own_width):
+                    start = b * WIDTH + y * own_width + at
+                    spread[y, tile * CORE_ROWS : (tile + 1) * CORE_ROWS, to : to + size] = words[
+                        :, start : start + size
+                    ]
+            spread[y, TILES * SLOTS : BLOCK, :] = tail
+        here = lax.axis_index("virt") // LAYERS
+        for hop, out in enumerate(outs):
+            out[...] = spread[lax.rem(here + hop, CHIPS)]
 
 
 def piece(group, b):
@@ -256,24 +277,56 @@
     return 8 * (index // 12), OWN_A * (index % 12)
 
 
-def column_kernel(own_ref, one_ref, two_ref, three_ref, out_ref, values, words):
-    add_words(one_ref, values, own_ref)
-    add_words(two_ref, values, values)
-    add_words(three_ref, values, values)
-    write_words(values, (words,))
-    code = words[:, WORDS : WORDS + 8]
+def column_kernel(own_ref, one_ref, two_ref, three_ref, out_ref, high, low, words):
+    core = lax.axis_index("pair") % CORES
+    parts = (own_ref, one_ref, two_ref, three_ref)
+    factors = [[scale_down(part[TILES * SLOTS : BLOCK, q : q + 1]) for q in range(CHIPS)] for part in parts]
+    tops = [None] * CHIPS
+    for tile in range(TILES):
+        q = tile % CHIPS
+        rows = slice(tile * SLOTS, (tile + 1) * SLOTS)
+        word = [part[rows, :] for part in parts]
+        high[rows, :] = sum(high_of(w) * f[q] for w, f in zip(word, factors))
+        low[rows, :] = sum(low_of(w) * f[q] for w, f in zip(word, factors))
+        top = jnp.maximum(jnp.abs(high[rows, :]), jnp.abs(low[rows, :]))
+        tops[q] = top if tops[q] is None else jnp.maximum(tops[q], top)
+    tops = [jnp.max(top, axis=1, keepdims=True) for top in tops]
+    every = functools.reduce(jnp.maximum, tops)
+    codes = [scale_code(jnp.where(core == 0, every, top)) for top in tops]
+    ups = [scale_up(code) for code in codes]
+    for tile in range(TILES):
+        rows = slice(tile * SLOTS, (tile + 1) * SLOTS)
+        words[rows, :] = joined(high[rows, :], low[rows, :], ups[tile % CHIPS])
     lane = iota((8, 8), 1)
-    tail = jnp.where(lane == 0, code[0:8], jnp.where(lane == 1, code[8:16], code[16:24]))
-    for j in range(COLUMNS):
+    tails = [jnp.where(lane == 0, code[0:8], jnp.where(lane == 1, code[8:16], code[16:24])) for code in codes]
+
+    def message(j, tail, place):
         for group in range(SLOTS // 8):
             for b in range(HALF):
                 row, lane_at = piece(group, b)
-                start = b * WIDTH + j * OWN_A
-                out_ref[j, row : row + 8, lane_at : lane_at + OWN_A] = words[
-                    group * 8 : group * 8 + 8, start : start + OWN_A
-                ]
+                start, base, pitch = place(b)
+                for at, tile, lane, size in crossing(start, OWN_A):
+                    source = base + tile * pitch + group * 8
+                    out_ref[j, row : row + 8, lane_at + at : lane_at + at + size] = words[
+                        source : source + 8, lane : lane + size
+                    ]
         out_ref[j, 0:8, 120:128] = tail
         out_ref[j, 8:16, 120:128] = tail
+
+    @pl.when(core == 0)
+    def _():
+        for j in range(COLUMNS):
+            message(j, tails[0], lambda b: (b * WIDTH + j * OWN_A, 0, SLOTS))
+
+    @pl.when(core == 1)
+    def _():
+        for x in range(CHIPS):
+            for z in range(LAYERS):
+                message(
+                    x * LAYERS + z,
+                    tails[x],
+                    lambda b: (b * (WIDTH // CHIPS) + z * OWN_A, x * SLOTS, CORE_ROWS),
+                )
 
 
 def final_kernel(round_ref, virt_s, tile_s, pairs_v, got_ref, out_ref, flat):
@@ -309,6 +362,26 @@
         out_ref[a] = jnp.where(keep, out_ref[a], 0.0)
 
 
+def device(x, core, y, z):
+    return ((x * CORES + core) * CHIPS + y) * LAYERS + z
+
+
+def hop_pairs(hop):
+    pairs = []
+    for x in range(CHIPS):
+        for y in range(CHIPS):
+            for z in range(LAYERS):
+                pairs.append((device(x, 0, y, z), device((x + hop) % CHIPS, 0, y, z)))
+                pairs.append((device(x, 1, y, z), device(x, 1, (y + hop) % CHIPS, z)))
+    return pairs
+
+
+def column_groups():
+    along = [(k, z) for k in range(CHIPS) for z in range(LAYERS)]
+    first = [[device(x, 0, y, z) for y, z in along] for x in range(CHIPS)]
+    return first + [[device(x, 1, y, z) for x, z in along] for y in range(CHIPS)]
+
+
 def shape(dims, dtype):
     return jax.ShapeDtypeStruct(dims, dtype)
 
@@ -354,59 +427,54 @@
     left = pltpu.VMEM((CORE_ROWS, DEPTH_PAD), F32)
     table = pltpu.VMEM((PAIRS_B, CORE_ROWS, PAIR), F32)
     work = [left, pltpu.VMEM((FAR, DEPTH, PAIR), BF16), pltpu.SemaphoreType.DMA]
-    message = shape((SLOTS, MESSAGE), I32)
     send = pl.pallas_call(
         send_kernel,
-        out_shape=[message, shape((REST, MESSAGE), I32)],
+        out_shape=shape((CORE_ROWS, MESSAGE), I32),
         in_specs=[VMEM, VMEM, HBM],
-        out_specs=[VMEM] * 2,
+        out_specs=VMEM,
         scratch_shapes=[*work, table],
         compiler_params=params(),
         name="send_rows",
     )(amp, near, far)
-    got = [lax.ppermute(part, "pair", [(i, i ^ 1) for i in range(OWNERS)]) for part in send]
+    got = lax.ppermute(send, "pair", [(i, i ^ 1) for i in range(OWNERS)])
     keep = pl.pallas_call(
         keep_kernel,
-        out_shape=[shape((PAIRS_B, SLOTS, PAIR), F32), shape((PAIRS_B, REST, PAIR), F32)],
+        out_shape=shape((PAIRS_B, CORE_ROWS, PAIR), F32),
         in_specs=[VMEM, VMEM, HBM],
-        out_specs=[VMEM] * 2,
+        out_specs=VMEM,
         scratch_shapes=work,
         compiler_params=params(),
         name="keep_rows",
         cost_estimate=pl.CostEstimate(flops=1 << 29, bytes_accessed=8 << 20, transcendentals=0),
     )(amp, near, far)
-    two = pl.pallas_call(
-        two_kernel,
-        out_shape=message,
+    own, one, two, three = pl.pallas_call(
+        chip_kernel,
+        out_shape=[shape((BLOCK, 128), I32)] * 4,
         in_specs=[VMEM] * 2,
-        out_specs=VMEM,
-        scratch_shapes=[pltpu.VMEM((PAIRS_B, SLOTS, PAIR), F32)],
-        compiler_params=params(),
-        name="chip_sum_two",
-    )(keep[0], got[0])
-    one, three, own = pl.pallas_call(
-        near_kernel,
-        out_shape=[message, message, shape((PAIRS_B, SLOTS, PAIR), F32)],
-        in_specs=[VMEM] * 2,
-        out_specs=[VMEM] * 3,
-        scratch_shapes=[pltpu.VMEM((PAIRS_B, REST, PAIR), F32)],
-        compiler_params=params(),
-        name="chip_sum_near",
-    )(keep[1], got[1])
-    hops = [
-        lax.ppermute(part, "pair", [(i, (i + CORES * hop) % OWNERS) for i in range(OWNERS)])
-        for hop, part in ((2, two), (1, one), (3, three))
+        out_specs=[VMEM] * 4,
+        scratch_shapes=[
+            table,
+            pltpu.VMEM((CORE_ROWS, MESSAGE), I32),
+            pltpu.VMEM((CHIPS, BLOCK, 128), I32),
+        ],
+        compiler_params=params(),
+        name="chip_sum",
+    )(keep, got)
+    two, one, three = [
+        lax.ppermute(part, ("pair", "virt"), hop_pairs(hop)) for hop, part in ((2, two), (1, one), (3, three))
     ]
     parts = pl.pallas_call(
         column_kernel,
         out_shape=shape((COLUMNS, 16, 128), I32),
         in_specs=[VMEM] * 4,
         out_specs=VMEM,
-        scratch_shapes=[pltpu.VMEM((PAIRS_B, SLOTS, PAIR), F32), pltpu.VMEM((SLOTS, MESSAGE), I32)],
+        scratch_shapes=[pltpu.VMEM((TILES * SLOTS, 128), t) for t in (F32, F32, I32)],
         compiler_params=params(),
         name="column_sum",
-    )(own, *hops)
-    back = lax.all_to_all(parts, "virt", split_axis=0, concat_axis=0, tiled=True)
+    )(own, one, two, three)
+    back = lax.all_to_all(
+        parts, ("pair", "virt"), split_axis=0, concat_axis=0, tiled=True, axis_index_groups=column_groups()
+    )
     return pl.pallas_call(
         final_kernel,
         out_shape=pltpu.HBM((OWN_A, TILE, ROWS), F32),

time: 62.7 us -> 58.7 us (0.936)
  waiting for transfers between devices: 22.7 us -> 19.9 us
  starting transfers between devices: 20.5 us -> 19.5 us
    ppermute x5 -> x4, waiting for transfers between devices: 11.7 us -> 9.71 us  [the longest x3 8.84 us: one_round(): lax.ppermute(part, ('pair', 'virt'), hop_pairs(hop))]
    ppermute x5 -> x4, starting transfers between devices: 4.25 us -> 3.18 us  [the longest x3 2.96 us: one_round(): lax.ppermute(part, ('pair', 'virt'), hop_pairs(hop))]
    all_to_all x1, waiting for transfers between devices: 10.9 us -> 10.2 us  [one_round(): lax.all_to_all(parts, ('pair', 'virt'), split_axis=0, concat_axis=0, tile...]
    pallas_call x4 -> x3, Pallas kernels: 4.75 us -> 4.79 us  [the longest x1 2.43 us: one_round(): pl.pallas_call(send_kernel, out_shape=shape((CORE_ROWS, MESSAGE), I32), i...]
  transfers between devices with their start and end apart: 7 -> 6, of which waited for: 5 -> 5; matrix products, arithmetic and copies ran while one was open for 1% -> 2% of each run, Pallas kernels for 13% -> 12%
where the time goes in v3:
time: 58.7 us; the launch traced here: 58.2 us
  waiting for transfers between devices  19.9 us (34%)
  starting transfers between devices  19.5 us (33%)
  Pallas kernels  17.1 us (29%)
  other arithmetic  0.85 us (1%)
  between operations  0.77 us (1%)
    all_to_all x1, starting transfers between devices, one_round(): lax.all_to_all(parts, ('pair', 'virt'), split_axis=0, concat_axis=0, tile...  10.7 us
    all_to_all x1, waiting for transfers between devices, one_round(): lax.all_to_all(parts, ('pair', 'virt'), split_axis=0, concat_axis=0, tile...  10.2 us
    ppermute x3, waiting for transfers between devices, one_round(): lax.ppermute(part, ('pair', 'virt'), hop_pairs(hop))  8.84 us
    pallas_call x1, Pallas kernels, masked_integrals(): pl.pallas_call(mask_kernel, out_shape=[pltpu.VMEM((NEAR, DEPTH, PAIR), BF...  5.68 us
    all_to_all x1, starting transfers between devices, one_round(): lax.all_to_all(packed, 'pair', split_axis=0, concat_axis=0, tiled=True)  5.54 us
    ppermute x3, starting transfers between devices, one_round(): lax.ppermute(part, ('pair', 'virt'), hop_pairs(hop))  2.96 us
    pallas_call x1, Pallas kernels, one_round(): pl.pallas_call(pack_kernel, out_shape=shape((OWNERS, SLOTS, DEPTH_PAD), B...  2.62 us
    pallas_call x1, Pallas kernels, one_round(): pl.pallas_call(send_kernel, out_shape=shape((CORE_ROWS, MESSAGE), I32), i...  2.43 us
  transfers between devices with their start and end apart: 6, of which 5 were waited for; matrix products, arithmetic and copies ran while one was open for 2% of the time, Pallas kernels for 12%

profile of v3, /device:TPU:6, one launch (start us, length us, event | category | flops | bytes accessed | tf_op | source)
XLA Modules:
  0.0 58.2 jit_solution(1886619423271406564)
XLA Ops:
  0.0 2.6 %pack.2 = bf16[8,24,512]{2,1,0:T(8,128)(2,1)} custom-call(s32[1]{0:T(128)} %constant.16.clone.1.round_ref, s32[320]{0:T(512)} %virt_s.5, s32[320]{0:T(512)} %virt_s.5, s32[640]{0:T(1024)} %pairs_v.3, bf16[10,80,320]{2,1,0:T(8,128)(2,1)} %bitcast.8), custom_call_target="tpu_custom_call" | custom-call | tf_op jit(solution)/shard_map/pack/pallas_call | solution.py:412
  2.6 5.5 %all-to-all-start.2 = ((bf16[8,24,512]{2,1,0:T(8,128)(2,1)}), bf16[8,24,512]{2,1,0:T(8,128)(2,1)S(1)}, u32[]{:S(2)}, u32[]{:S(2)}) async-start(bf16[8,24,512]{2,1,0:T(8,128)(2,1)} %pack.2), calls=%async_computation.2 | async-start | bytes 393216 | tf_op jit(solution)/shard_map/all_to_all | solution.py:424
  8.2 5.7 %mask_turn.2 = (bf16[6,400,640]{2,1,0:T(8,128)(2,1)S(1)}, bf16[2,400,640]{2,1,0:T(8,128)(2,1)}) custom-call(s32[1]{0:T(128)} %constant.16.clone.1.round_ref, s32[320]{0:T(512)} %virt_s.5, s32[16]{0:T(128)} %tile_s.3, s32[320]{0:T(512)} %virt_s.5, bf16[10,40,16,320]{3,2,1,0:T(8,128)(2,1)} %int_hbm.1), custom_call_target="tpu_custom_call" | custom-call | flops 1073741824 | bytes 10485760 | tf_op jit(solution)/shard_map/mask_turn/pallas_call | solution.py:390
  13.8 0.0 all-to-all-done.2.amp_ref
  13.9 2.4 %send_rows.2 = s32[96,2688]{1,0:T(8,128)S(1)} custom-call(bf16[8,24,512]{2,1,0:T(8,128)(2,1)S(1)} %all-to-all-done.2.amp_ref, bf16[6,400,640]{2,1,0:T(8,128)(2,1)S(1)} %get-tuple-element.60.near_ref, bf16[2,400,640]{2,1,0:T(8,128)(2,1)} %get-tuple-element.61.far_hbm), custom_call_target="tpu_custom_call" | custom-call | tf_op jit(solution)/shard_map/send_rows/pallas_call | solution.py:430
  16.3 0.2 collective-permute-start.4
  16.5 1.6 %keep_rows.2.keep_ref = f32[8,96,640]{2,1,0:T(8,128)S(1)} custom-call(bf16[8,24,512]{2,1,0:T(8,128)(2,1)S(1)} %all-to-all-done.2.amp_ref, bf16[6,400,640]{2,1,0:T(8,128)(2,1)S(1)} %get-tuple-element.60.near_ref, bf16[2,400,640]{2,1,0:T(8,128)(2,1)} %get-tuple-element.61.far_hbm), custom_call_target="tpu_custom_call" | custom-call | flops 536870912 | bytes 8388608 | tf_op jit(solution)/shard_map/keep_rows/pallas_call | solution.py:440
  18.1 0.0 copy-start.3
  18.1 0.0 copy-start.2
  18.1 0.0 copy-start.4
  18.2 0.9 %collective-permute-done.4.got_ref = s32[96,2688]{1,0:T(8,128)S(1)} collective-permute-done((s32[96,2688]{1,0:T(8,128)S(1)}, s32[96,2688]{1,0:T(8,128)S(1)}, u32[]{:S(2)}, u32[]{:S(2)}) %collective-permute-start.4) | collective-permute-done | bytes 1032224 | tf_op jit(solution)/shard_map/ppermute | solution.py:439
  19.0 0.8 %chip_sum.2 = (s32[504,128]{1,0:T(8,128)S(1)}, s32[504,128]{1,0:T(8,128)S(1)}, s32[504,128]{1,0:T(8,128)S(1)}, s32[504,128]{1,0:T(8,128)S(1)}) custom-call(f32[8,96,640]{2,1,0:T(8,128)S(1)} %keep_rows.2.keep_ref, s32[96,2688]{1,0:T(8,128)S(1)} %collective-permute-done.4.got_ref), custom_call_target="tpu_custom_call" | custom-call | tf_op jit(solution)/shard_map/chip_sum/pallas_call | solution.py:450
  19.8 1.2 %collective-permute-start.5 = (s32[504,128]{1,0:T(8,128)S(1)}, s32[504,128]{1,0:T(8,128)S(1)}, u32[]{:S(2)}, u32[]{:S(2)}) collective-permute-start(s32[504,128]{1,0:T(8,128)S(1)} %get-tuple-element.63), channel_id=1, source_target_pairs={{0,64},{32,40},{1,65},{33,41},{2,66},{34,42},{3,67},{35,43},{4,68}... | collective-permute-start | bytes 774152 | tf_op jit(solution)/shard_map/ppermute | solution.py:464
  21.0 1.8 %collective-permute-start.6 = (s32[504,128]{1,0:T(8,128)S(1)}, s32[504,128]{1,0:T(8,128)S(1)}, u32[]{:S(2)}, u32[]{:S(2)}) collective-permute-start(s32[504,128]{1,0:T(8,128)S(1)} %get-tuple-element.64), channel_id=1, source_target_pairs={{0,128},{32,48},{1,129},{33,49},{2,130},{34,50},{3,131},{35,51},{4... | collective-permute-start | bytes 774152 | tf_op jit(solution)/shard_map/ppermute | solution.py:464
  22.8 0.0 collective-permute-start.7
  22.8 3.4 %collective-permute-done.5.one_ref = s32[504,128]{1,0:T(8,128)S(1)} collective-permute-done((s32[504,128]{1,0:T(8,128)S(1)}, s32[504,128]{1,0:T(8,128)S(1)}, u32[]{:S(2)}, u32[]{:S(2)}) %collective-permute-start.5) | collective-permute-done | bytes 258080 | tf_op jit(solution)/shard_map/ppermute | solution.py:464
  26.2 2.7 %collective-permute-done.6.two_ref = s32[504,128]{1,0:T(8,128)S(1)} collective-permute-done((s32[504,128]{1,0:T(8,128)S(1)}, s32[504,128]{1,0:T(8,128)S(1)}, u32[]{:S(2)}, u32[]{:S(2)}) %collective-permute-start.6) | collective-permute-done | bytes 258080 | tf_op jit(solution)/shard_map/ppermute | solution.py:464
  28.9 2.7 %collective-permute-done.7.three_ref = s32[504,128]{1,0:T(8,128)S(1)} collective-permute-done((s32[504,128]{1,0:T(8,128)S(1)}, s32[504,128]{1,0:T(8,128)S(1)}, u32[]{:S(2)}, u32[]{:S(2)}) %collective-permute-start.7) | collective-permute-done | bytes 258080 | tf_op jit(solution)/shard_map/ppermute | solution.py:464
  31.6 2.1 %column_sum.2 = s32[32,16,128]{2,1,0:T(8,128)} custom-call(s32[504,128]{1,0:T(8,128)S(1)} %get-tuple-element.62.own_ref, s32[504,128]{1,0:T(8,128)S(1)} %collective-permute-done.5.one_ref, s32[504,128]{1,0:T(8,128)S(1)} %collective-permute-done.6.two_ref, s32[504,128]{1,0:T(8,128)S(1)} %collective-permute-done.7.three_ref), custom_call_target="tpu_custom_call" | custom-call | tf_op jit(solution)/shard_map/column_sum/pallas_call | solution.py:466
  33.7 10.7 %all-to-all-start.3 = ((s32[32,16,128]{2,1,0:T(8,128)}), s32[32,16,128]{2,1,0:T(8,128)S(1)}, u32[]{:S(2)}, u32[]{:S(2)}) async-start(s32[32,16,128]{2,1,0:T(8,128)} %column_sum.2), calls=%async_computation.3 | async-start | bytes 524288 | tf_op jit(solution)/shard_map/all_to_all | solution.py:475
  44.4 0.0 copy-done.3
  44.4 0.1 eq.15
  44.5 0.2 convert_reduce_fusion
  44.7 0.6 %reduce_max.9 = s32[]{:T(128)} reduce(s32[8,8]{1,0:T(8,128)S(1)} %convert_reduce_fusion, s32[]{:T(128)} %constant.18.clone.1), dimensions={0,1}, to_apply=%region_1.0 | reduce | flops 63 | bytes 264 | tf_op jit(solution)/shard_map/reduce_max | solution.py:501
  46.0 10.2 %all-to-all-done.3.got_ref = s32[32,16,128]{2,1,0:T(8,128)S(1)} async-done(((s32[32,16,128]{2,1,0:T(8,128)}), s32[32,16,128]{2,1,0:T(8,128)S(1)}, u32[]{:S(2)}, u32[]{:S(2)}) %all-to-all-start.3) | async-done | bytes 262176 | tf_op jit(solution)/shard_map/all_to_all | solution.py:475
  56.2 0.0 copy-done.2
  56.2 0.0 copy-done.4
  56.3 1.9 %unpack.2 = f32[10,16,80]{2,1,0:T(8,128)} custom-call(s32[1]{0:T(128)} %constant.16.clone.1.round_ref, s32[320]{0:T(512)S(1)} %copy-done.2, s32[16]{0:T(128)S(1)} %copy-done.4, s32[640]{0:T(1024)S(1)} %copy-done.3, s32[32,16,128]{2,1,0:T(8,128)S(1)} %all-to-all-done.3.got_ref), custom_call_target="tpu_custom_call" | custom-call | tf_op jit(solution)/shard_map/unpack/pallas_call | solution.py:478
  (1 shorter events, 0.0 us)
Async XLA Ops:
  2.6 11.2 %all-to-all-start.2 = ((bf16[8,24,512]{2,1,0:T(8,128)(2,1)}), bf16[8,24,512]{2,1,0:T(8,128)(2,1)S(1)}, u32[]{:S(2)}, u32[]{:S(2)}) async-start(bf16[8,24,512]{2,1,0:T(8,128)(2,1)} %pack.2), calls=%async_computation.2 | async-start | bytes 393216 | tf_op jit(solution)/shard_map/all_to_all | solution.py:424
  16.3 2.7 %collective-permute-start.4 = (s32[96,2688]{1,0:T(8,128)S(1)}, s32[96,2688]{1,0:T(8,128)S(1)}, u32[]{:S(2)}, u32[]{:S(2)}) collective-permute-start(s32[96,2688]{1,0:T(8,128)S(1)} %send_rows.2), channel_id=1, source_target_pairs={{0,32},{32,0},{64,96},{96,64},{128,160},{160,128},{192,224},{224,1... | collective-permute-start | bytes 3096584 | tf_op jit(solution)/shard_map/ppermute | solution.py:439
  18.1 26.3 %copy-start.3 = (s32[640]{0:T(1024)S(1)}, s32[640]{0:T(1024)}, u32[]{:S(2)}) copy-start(s32[640]{0:T(1024)} %pairs_v.3) | copy-start | bytes 7684
  18.1 38.1 %copy-start.2 = (s32[320]{0:T(512)S(1)}, s32[320]{0:T(512)}, u32[]{:S(2)}) copy-start(s32[320]{0:T(512)} %virt_s.5) | copy-start | bytes 3844
  18.1 38.1 %copy-start.4 = (s32[16]{0:T(128)S(1)}, s32[16]{0:T(128)}, u32[]{:S(2)}) copy-start(s32[16]{0:T(128)} %tile_s.3) | copy-start | bytes 196
  19.8 6.4 %collective-permute-start.5 = (s32[504,128]{1,0:T(8,128)S(1)}, s32[504,128]{1,0:T(8,128)S(1)}, u32[]{:S(2)}, u32[]{:S(2)}) collective-permute-start(s32[504,128]{1,0:T(8,128)S(1)} %get-tuple-element.63), channel_id=1, source_target_pairs={{0,64},{32,40},{1,65},{33,41},{2,66},{34,42},{3,67},{35,43},{4,68}... | collective-permute-start | bytes 774152 | tf_op jit(solution)/shard_map/ppermute | solution.py:464
  21.0 7.9 %collective-permute-start.6 = (s32[504,128]{1,0:T(8,128)S(1)}, s32[504,128]{1,0:T(8,128)S(1)}, u32[]{:S(2)}, u32[]{:S(2)}) collective-permute-start(s32[504,128]{1,0:T(8,128)S(1)} %get-tuple-element.64), channel_id=1, source_target_pairs={{0,128},{32,48},{1,129},{33,49},{2,130},{34,50},{3,131},{35,51},{4... | collective-permute-start | bytes 774152 | tf_op jit(solution)/shard_map/ppermute | solution.py:464
  22.8 8.8 %collective-permute-start.7 = (s32[504,128]{1,0:T(8,128)S(1)}, s32[504,128]{1,0:T(8,128)S(1)}, u32[]{:S(2)}, u32[]{:S(2)}) collective-permute-start(s32[504,128]{1,0:T(8,128)S(1)} %get-tuple-element.65), channel_id=1, source_target_pairs={{0,192},{32,56},{1,193},{33,57},{2,194},{34,58},{3,195},{35,59},{4... | collective-permute-start | bytes 774152 | tf_op jit(solution)/shard_map/ppermute | solution.py:464
  33.7 22.6 %all-to-all-start.3 = ((s32[32,16,128]{2,1,0:T(8,128)}), s32[32,16,128]{2,1,0:T(8,128)S(1)}, u32[]{:S(2)}, u32[]{:S(2)}) async-start(s32[32,16,128]{2,1,0:T(8,128)} %column_sum.2), calls=%async_computation.3 | async-start | bytes 524288 | tf_op jit(solution)/shard_map/all_to_all | solution.py:475

commit v4 on v3

--- a/solution.py
+++ b/solution.py
@@ -100,9 +100,24 @@
 
 
 def mask_kernel(
-    round_ref, virt_s, tile_s, virt_v, int_hbm, near_ref, far_hbm, slabs, masks, turn, wide, far, sems, far_sems
+    round_ref,
+    virt_s,
+    tile_s,
+    virt_v,
+    pairs_v,
+    int_hbm,
+    near_ref,
+    far_hbm,
+    hot_ref,
+    keep_ref,
+    slabs,
+    masks,
+    turn,
+    wide,
+    far,
+    sems,
+    far_sems,
 ):
-    del round_ref
 
     def load(c):
         return pltpu.make_async_copy(int_hbm.at[c], slabs.at[c], sems.at[c])
@@ -113,7 +128,14 @@
 
     for c in range(OWN_C):
         load(c).start()
-    label = jnp.bitwise_xor(tile_column(tile_s), virt_v[...].reshape(1, WIDTH))
+    row = local_labels(pairs_v)
+    _, hot = slots_of(row, round_ref[0])
+    hot_ref[...] = hot
+    column = tile_column(tile_s)
+    base_a = lax.axis_index("virt") * OWN_A
+    for a in range(OWN_A):
+        keep_ref[a] = jnp.where(jnp.bitwise_xor(column, virt_s[base_a + a]) == row, 1.0, 0.0)
+    label = jnp.bitwise_xor(column, virt_v[...].reshape(1, WIDTH))
     for g in range(8):
         masks[g] = jnp.where(label == g, 1.0, 0.0).astype(BF16)
     high, low = iota((256, 256), 0), iota((256, 256), 1)
@@ -190,15 +212,13 @@
     return jnp.right_shift(jnp.left_shift(word, 16), 16).astype(F32)
 
 
-def row_largest(values):
-    top = jnp.abs(values[0])
-    for pair in range(1, PAIRS_B):
-        top = jnp.maximum(top, jnp.abs(values[pair]))
-    return jnp.max(top, axis=1, keepdims=True)
-
-
-def write_words(values, out_ref):
-    code = scale_code(row_largest(values))
+def folded(value):
+    value = jnp.abs(value)
+    return functools.reduce(jnp.maximum, [value[:, at : at + 128] for at in range(0, PAIR, 128)])
+
+
+def write_words(values, top, out_ref):
+    code = scale_code(jnp.max(top, axis=1, keepdims=True))
     factor = scale_up(code)
     for pair in range(PAIRS_B // 2):
         out_ref[:, pair * PAIR : (pair + 1) * PAIR] = joined(values[pair], values[pair + PAIRS_B // 2], factor)
@@ -206,11 +226,15 @@
 
 
 def send_kernel(amp_ref, near_ref, far_hbm, out_ref, left, far, sem, values):
+    tops = []
+
     def put(pair, value):
         values[pair] = value
+        top = folded(value)
+        tops.append(jnp.maximum(tops[-1], top) if tops else top)
 
     products(1 - lax.axis_index("pair") % CORES, amp_ref, near_ref, far_hbm, left, far, sem, put)
-    write_words(values, out_ref)
+    write_words(values, tops[-1], out_ref)
 
 
 def keep_kernel(amp_ref, near_ref, far_hbm, out_ref, left, far, sem):
@@ -221,12 +245,16 @@
 
 
 def add_words(words, values, start):
+    top = None
     factor = scale_down(words[:, WORDS : WORDS + 1])
     for pair in range(PAIRS_B // 2):
         word = words[:, pair * PAIR : (pair + 1) * PAIR]
         other = pair + PAIRS_B // 2
-        values[pair] = start[pair] + high_of(word) * factor
-        values[other] = start[other] + low_of(word) * factor
+        for at, part in ((pair, high_of(word)), (other, low_of(word))):
+            value = start[at] + part * factor
+            values[at] = value
+            top = folded(value) if top is None else jnp.maximum(top, folded(value))
+    return top
 
 
 def crossing(start, length):
@@ -239,11 +267,11 @@
     return cuts
 
 
-def chip_kernel(keep_ref, got_ref, own_ref, one_ref, two_ref, three_ref, values, words, spread):
+def chip_kernel(keep_ref, got_ref, own_ref, one_ref, three_ref, two_ref, values, words, spread):
     core = lax.axis_index("pair") % CORES
     outs = (own_ref, one_ref, two_ref, three_ref)
-    add_words(got_ref, values, keep_ref)
-    write_words(values, words)
+    top = add_words(got_ref, values, keep_ref)
+    write_words(values, top, words)
 
     @pl.when(core == 0)
     def _():
@@ -277,7 +305,7 @@
     return 8 * (index // 12), OWN_A * (index % 12)
 
 
-def column_kernel(own_ref, one_ref, two_ref, three_ref, out_ref, high, low, words):
+def column_kernel(own_ref, one_ref, three_ref, two_ref, out_ref, high, low, words):
     core = lax.axis_index("pair") % CORES
     parts = (own_ref, one_ref, two_ref, three_ref)
     factors = [[scale_down(part[TILES * SLOTS : BLOCK, q : q + 1]) for q in range(CHIPS)] for part in parts]
@@ -329,9 +357,7 @@
                 )
 
 
-def final_kernel(round_ref, virt_s, tile_s, pairs_v, got_ref, out_ref, flat):
-    row = local_labels(pairs_v)
-    _, hot = slots_of(row, round_ref[0])
+def final_kernel(hot_ref, keep_ref, got_ref, out_ref, flat):
     lane = iota((8, 128), 1)
     sums = [[jnp.zeros((8, 128), F32) for _ in range(2)] for _ in range(2)]
     for j in range(COLUMNS):
@@ -351,15 +377,12 @@
                 to = (half * HALF + b) * OWN_A
                 flat[group * 8 : group * 8 + 8, to : to + OWN_A] = sums[half][at // 8][:, lane_at : lane_at + OWN_A]
     spread = lax.dot_general(
-        flat[...], hot, (((0,), (0,)), ((), ())), precision=lax.Precision.HIGHEST, preferred_element_type=F32
+        flat[...], hot_ref[...], (((0,), (0,)), ((), ())), precision=lax.Precision.HIGHEST, preferred_element_type=F32
     )
-    base = lax.axis_index("virt") * OWN_A
-    column = tile_column(tile_s)
     for a in range(OWN_A):
         for b in range(TILE):
             out_ref[a, b : b + 1, :] = spread[b * OWN_A + a : b * OWN_A + a + 1]
-        keep = jnp.bitwise_xor(column, virt_s[base + a]) == row
-        out_ref[a] = jnp.where(keep, out_ref[a], 0.0)
+        out_ref[a] = jnp.where(keep_ref[a] > 0.0, out_ref[a], 0.0)
 
 
 def device(x, core, y, z):
@@ -386,12 +409,17 @@
     return jax.ShapeDtypeStruct(dims, dtype)
 
 
-def masked_integrals(number, integrals, virt, tile):
+def masked_integrals(number, integrals, virt, tile, pairs):
     return pl.pallas_call(
         mask_kernel,
-        out_shape=[pltpu.VMEM((NEAR, DEPTH, PAIR), BF16), pltpu.HBM((FAR, DEPTH, PAIR), BF16)],
-        in_specs=[SMEM, SMEM, SMEM, VMEM, HBM],
-        out_specs=[VMEM, HBM],
+        out_shape=[
+            pltpu.VMEM((NEAR, DEPTH, PAIR), BF16),
+            pltpu.HBM((FAR, DEPTH, PAIR), BF16),
+            shape((SLOTS, ROWS), F32),
+            shape((OWN_A, TILE, ROWS), F32),
+        ],
+        in_specs=[SMEM, SMEM, SMEM, VMEM, VMEM, HBM],
+        out_specs=[VMEM, HBM, VMEM, VMEM],
         scratch_shapes=[
             pltpu.VMEM((OWN_C, OWN_D, TILE, WIDTH), BF16),
             pltpu.VMEM((8, TILE, WIDTH), BF16),
@@ -404,7 +432,7 @@
         compiler_params=params(),
         name="mask_turn",
         cost_estimate=pl.CostEstimate(flops=1 << 30, bytes_accessed=10 << 20, transcendentals=0),
-    )(number, virt, tile, virt, pltpu.with_memory_space_constraint(integrals, pltpu.HBM))
+    )(number, virt, tile, virt, pairs, pltpu.with_memory_space_constraint(integrals, pltpu.HBM))
 
 
 def one_round(round_index, amplitudes, integrals, virt, tile, pairs):
@@ -422,7 +450,7 @@
         name="pack",
     )(number, virt, virt, pairs, pltpu.with_memory_space_constraint(jnp.transpose(amplitudes, (1, 0, 2)), pltpu.HBM))
     amp = lax.all_to_all(packed, "pair", split_axis=0, concat_axis=0, tiled=True)
-    near, far = masked_integrals(number, integrals, virt, tile)
+    near, far, hot, valid = masked_integrals(number, integrals, virt, tile, pairs)
     far = pltpu.with_memory_space_constraint(far, pltpu.HBM)
     left = pltpu.VMEM((CORE_ROWS, DEPTH_PAD), F32)
     table = pltpu.VMEM((PAIRS_B, CORE_ROWS, PAIR), F32)
@@ -447,7 +475,7 @@
         name="keep_rows",
         cost_estimate=pl.CostEstimate(flops=1 << 29, bytes_accessed=8 << 20, transcendentals=0),
     )(amp, near, far)
-    own, one, two, three = pl.pallas_call(
+    own, one, three, two = pl.pallas_call(
         chip_kernel,
         out_shape=[shape((BLOCK, 128), I32)] * 4,
         in_specs=[VMEM] * 2,
@@ -460,8 +488,8 @@
         compiler_params=params(),
         name="chip_sum",
     )(keep, got)
-    two, one, three = [
-        lax.ppermute(part, ("pair", "virt"), hop_pairs(hop)) for hop, part in ((2, two), (1, one), (3, three))
+    one, three, two = [
+        lax.ppermute(part, ("pair", "virt"), hop_pairs(hop)) for hop, part in ((1, one), (3, three), (2, two))
     ]
     parts = pl.pallas_call(
         column_kernel,
@@ -471,19 +499,19 @@
         scratch_shapes=[pltpu.VMEM((TILES * SLOTS, 128), t) for t in (F32, F32, I32)],
         compiler_params=params(),
         name="column_sum",
-    )(own, one, two, three)
+    )(own, one, three, two)
     back = lax.all_to_all(
         parts, ("pair", "virt"), split_axis=0, concat_axis=0, tiled=True, axis_index_groups=column_groups()
     )
     return pl.pallas_call(
         final_kernel,
         out_shape=pltpu.HBM((OWN_A, TILE, ROWS), F32),
-        in_specs=[SMEM, SMEM, SMEM, VMEM, VMEM],
+        in_specs=[VMEM] * 3,
         out_specs=VMEM,
         scratch_shapes=[pltpu.VMEM((SLOTS, TILE * OWN_A), F32)],
         compiler_params=params(),
         name="unpack",
-    )(number, virt, tile, pairs, back)
+    )(hot, valid, back)
 
 
 def body(amplitudes, integrals, virt_irrep, tile_irrep, pair_irrep):

time: 58.7 us -> 58.1 us (0.990)
  the two profiles are of different devices: /device:TPU:6 before, /device:TPU:1 now
where the time goes in v4:
time: 58.1 us; the launch traced here: 57.6 us
  starting transfers between devices  21.6 us (37%)
  Pallas kernels  17.5 us (30%)
  waiting for transfers between devices  16.9 us (29%)
  other arithmetic  0.85 us (1%)
  between operations  0.76 us (1%)
    all_to_all x1, starting transfers between devices, one_round(): lax.all_to_all(parts, ('pair', 'virt'), split_axis=0, concat_axis=0, tile...  10.3 us
    all_to_all x1, waiting for transfers between devices, one_round(): lax.all_to_all(parts, ('pair', 'virt'), split_axis=0, concat_axis=0, tile...  9.89 us
    all_to_all x1, starting transfers between devices, one_round(): lax.all_to_all(packed, 'pair', split_axis=0, concat_axis=0, tiled=True)  6.53 us
    ppermute x3, waiting for transfers between devices, one_round(): lax.ppermute(part, ('pair', 'virt'), hop_pairs(hop))  6.31 us
    pallas_call x1, Pallas kernels, masked_integrals(): pl.pallas_call(mask_kernel, out_shape=[pltpu.VMEM((NEAR, DEPTH, PAIR), BF...  5.86 us
    ppermute x3, starting transfers between devices, one_round(): lax.ppermute(part, ('pair', 'virt'), hop_pairs(hop))  3.71 us
    pallas_call x1, Pallas kernels, one_round(): pl.pallas_call(pack_kernel, out_shape=shape((OWNERS, SLOTS, DEPTH_PAD), B...  2.61 us
    pallas_call x1, Pallas kernels, one_round(): pl.pallas_call(send_kernel, out_shape=shape((CORE_ROWS, MESSAGE), I32), i...  2.42 us
  transfers between devices with their start and end apart: 6, of which 5 were waited for; matrix products, arithmetic and copies ran while one was open for 2% of the time, Pallas kernels for 13%

profile of v4, /device:TPU:1, one launch (start us, length us, event | category | flops | bytes accessed | tf_op | source)
XLA Modules:
  0.0 57.6 jit_solution(18074008369938742065)
XLA Ops:
  0.0 2.6 %pack.2 = bf16[8,24,512]{2,1,0:T(8,128)(2,1)} custom-call(s32[1]{0:T(128)} %constant.16.clone.1.round_ref, s32[320]{0:T(512)} %virt_v.3, s32[320]{0:T(512)} %virt_v.3, s32[640]{0:T(1024)} %pairs_v.3, bf16[10,80,320]{2,1,0:T(8,128)(2,1)} %bitcast.8), custom_call_target="tpu_custom_call" | custom-call | tf_op jit(solution)/shard_map/pack/pallas_call | solution.py:440
  2.6 6.5 %all-to-all-start.2 = ((bf16[8,24,512]{2,1,0:T(8,128)(2,1)}), bf16[8,24,512]{2,1,0:T(8,128)(2,1)S(1)}, u32[]{:S(2)}, u32[]{:S(2)}) async-start(bf16[8,24,512]{2,1,0:T(8,128)(2,1)} %pack.2), calls=%async_computation.2 | async-start | bytes 393216 | tf_op jit(solution)/shard_map/all_to_all | solution.py:452
  9.1 5.9 %mask_turn.2 = (bf16[6,400,640]{2,1,0:T(8,128)(2,1)S(1)}, bf16[2,400,640]{2,1,0:T(8,128)(2,1)}, f32[24,80]{1,0:T(8,128)S(1)}, f32[10,16,80]{2,1,0:T(8,128)S(1)}) custom-call(s32[1]{0:T(128)} %constant.16.clone.1.round_ref, s32[320]{0:T(512)} %virt_v.3, s32[16]{0:T(128)} %tile_s.1, s32[320]{0:T(512)} %virt_v.3, s32[640]{0:T(1024)} %pairs_v.3, ...), custom_call_target="tpu_custom_call" | custom-call | flops 1073741824 | bytes 10485760 | tf_op jit(solution)/shard_map/mask_turn/pallas_call | solution.py:413
  15.0 0.0 all-to-all-done.2.amp_ref
  15.1 2.4 %send_rows.2 = s32[96,2688]{1,0:T(8,128)S(1)} custom-call(bf16[8,24,512]{2,1,0:T(8,128)(2,1)S(1)} %all-to-all-done.2.amp_ref, bf16[6,400,640]{2,1,0:T(8,128)(2,1)S(1)} %get-tuple-element.66.near_ref, bf16[2,400,640]{2,1,0:T(8,128)(2,1)} %get-tuple-element.67.far_hbm), custom_call_target="tpu_custom_call" | custom-call | tf_op jit(solution)/shard_map/send_rows/pallas_call | solution.py:458
  17.5 1.0 %collective-permute-start.4 = (s32[96,2688]{1,0:T(8,128)S(1)}, s32[96,2688]{1,0:T(8,128)S(1)}, u32[]{:S(2)}, u32[]{:S(2)}) collective-permute-start(s32[96,2688]{1,0:T(8,128)S(1)} %send_rows.2), channel_id=1, source_target_pairs={{0,32},{32,0},{64,96},{96,64},{128,160},{160,128},{192,224},{224,1... | collective-permute-start | bytes 3096584 | tf_op jit(solution)/shard_map/ppermute | solution.py:467
  18.5 1.6 %keep_rows.2.keep_ref = f32[8,96,640]{2,1,0:T(8,128)S(1)} custom-call(bf16[8,24,512]{2,1,0:T(8,128)(2,1)S(1)} %all-to-all-done.2.amp_ref, bf16[6,400,640]{2,1,0:T(8,128)(2,1)S(1)} %get-tuple-element.66.near_ref, bf16[2,400,640]{2,1,0:T(8,128)(2,1)} %get-tuple-element.67.far_hbm), custom_call_target="tpu_custom_call" | custom-call | flops 536870912 | bytes 8388608 | tf_op jit(solution)/shard_map/keep_rows/pallas_call | solution.py:468
  20.1 0.0 copy-start.3
  20.1 0.0 copy-start.2
  20.2 0.0 copy-start.4
  20.2 0.6 %collective-permute-done.4.got_ref = s32[96,2688]{1,0:T(8,128)S(1)} collective-permute-done((s32[96,2688]{1,0:T(8,128)S(1)}, s32[96,2688]{1,0:T(8,128)S(1)}, u32[]{:S(2)}, u32[]{:S(2)}) %collective-permute-start.4) | collective-permute-done | bytes 1032224 | tf_op jit(solution)/shard_map/ppermute | solution.py:467
  20.8 1.6 %chip_sum.2 = (s32[504,128]{1,0:T(8,128)S(1)}, s32[504,128]{1,0:T(8,128)S(1)}, s32[504,128]{1,0:T(8,128)S(1)}, s32[504,128]{1,0:T(8,128)S(1)}) custom-call(f32[8,96,640]{2,1,0:T(8,128)S(1)} %keep_rows.2.keep_ref, s32[96,2688]{1,0:T(8,128)S(1)} %collective-permute-done.4.got_ref), custom_call_target="tpu_custom_call" | custom-call | tf_op jit(solution)/shard_map/chip_sum/pallas_call | solution.py:478
  22.4 0.6 %collective-permute-start.5 = (s32[504,128]{1,0:T(8,128)S(1)}, s32[504,128]{1,0:T(8,128)S(1)}, u32[]{:S(2)}, u32[]{:S(2)}) collective-permute-start(s32[504,128]{1,0:T(8,128)S(1)} %get-tuple-element.69), channel_id=1, source_target_pairs={{0,64},{32,40},{1,65},{33,41},{2,66},{34,42},{3,67},{35,43},{4,68}... | collective-permute-start | bytes 774152 | tf_op jit(solution)/shard_map/ppermute | solution.py:492
  23.0 2.1 %collective-permute-start.6 = (s32[504,128]{1,0:T(8,128)S(1)}, s32[504,128]{1,0:T(8,128)S(1)}, u32[]{:S(2)}, u32[]{:S(2)}) collective-permute-start(s32[504,128]{1,0:T(8,128)S(1)} %get-tuple-element.70), channel_id=1, source_target_pairs={{0,192},{32,56},{1,193},{33,57},{2,194},{34,58},{3,195},{35,59},{4... | collective-permute-start | bytes 774152 | tf_op jit(solution)/shard_map/ppermute | solution.py:492
  25.1 1.0 %collective-permute-start.7 = (s32[504,128]{1,0:T(8,128)S(1)}, s32[504,128]{1,0:T(8,128)S(1)}, u32[]{:S(2)}, u32[]{:S(2)}) collective-permute-start(s32[504,128]{1,0:T(8,128)S(1)} %get-tuple-element.71), channel_id=1, source_target_pairs={{0,128},{32,48},{1,129},{33,49},{2,130},{34,50},{3,131},{35,51},{4... | collective-permute-start | bytes 774152 | tf_op jit(solution)/shard_map/ppermute | solution.py:492
  26.1 3.0 %collective-permute-done.5.one_ref = s32[504,128]{1,0:T(8,128)S(1)} collective-permute-done((s32[504,128]{1,0:T(8,128)S(1)}, s32[504,128]{1,0:T(8,128)S(1)}, u32[]{:S(2)}, u32[]{:S(2)}) %collective-permute-start.5) | collective-permute-done | bytes 258080 | tf_op jit(solution)/shard_map/ppermute | solution.py:492
  29.1 2.0 %collective-permute-done.6.three_ref = s32[504,128]{1,0:T(8,128)S(1)} collective-permute-done((s32[504,128]{1,0:T(8,128)S(1)}, s32[504,128]{1,0:T(8,128)S(1)}, u32[]{:S(2)}, u32[]{:S(2)}) %collective-permute-start.6) | collective-permute-done | bytes 258080 | tf_op jit(solution)/shard_map/ppermute | solution.py:492
  31.2 1.2 %collective-permute-done.7.two_ref = s32[504,128]{1,0:T(8,128)S(1)} collective-permute-done((s32[504,128]{1,0:T(8,128)S(1)}, s32[504,128]{1,0:T(8,128)S(1)}, u32[]{:S(2)}, u32[]{:S(2)}) %collective-permute-start.7) | collective-permute-done | bytes 258080 | tf_op jit(solution)/shard_map/ppermute | solution.py:492
  32.4 2.1 %column_sum.2 = s32[32,16,128]{2,1,0:T(8,128)} custom-call(s32[504,128]{1,0:T(8,128)S(1)} %get-tuple-element.68.own_ref, s32[504,128]{1,0:T(8,128)S(1)} %collective-permute-done.5.one_ref, s32[504,128]{1,0:T(8,128)S(1)} %collective-permute-done.6.three_ref, s32[504,128]{1,0:T(8,128)S(1)} %collective-permute-done.7.two_ref), custom_call_target="tpu_custom_call" | custom-call | tf_op jit(solution)/shard_map/column_sum/pallas_call | solution.py:494
  34.5 10.3 %all-to-all-start.3 = ((s32[32,16,128]{2,1,0:T(8,128)}), s32[32,16,128]{2,1,0:T(8,128)S(1)}, u32[]{:S(2)}, u32[]{:S(2)}) async-start(s32[32,16,128]{2,1,0:T(8,128)} %column_sum.2), calls=%async_computation.3 | async-start | bytes 524288 | tf_op jit(solution)/shard_map/all_to_all | solution.py:503
  44.8 0.0 copy-done.3
  44.8 0.1 eq.15
  44.9 0.2 convert_reduce_fusion
  45.1 0.6 %reduce_max.9 = s32[]{:T(128)} reduce(s32[8,8]{1,0:T(8,128)S(1)} %convert_reduce_fusion, s32[]{:T(128)} %constant.18.clone.1), dimensions={0,1}, to_apply=%region_1.0 | reduce | flops 63 | bytes 264 | tf_op jit(solution)/shard_map/reduce_max | solution.py:529
  46.4 9.9 %all-to-all-done.3.got_ref = s32[32,16,128]{2,1,0:T(8,128)S(1)} async-done(((s32[32,16,128]{2,1,0:T(8,128)}), s32[32,16,128]{2,1,0:T(8,128)S(1)}, u32[]{:S(2)}, u32[]{:S(2)}) %all-to-all-start.3) | async-done | bytes 262176 | tf_op jit(solution)/shard_map/all_to_all | solution.py:503
  56.3 1.3 %unpack.2 = f32[10,16,80]{2,1,0:T(8,128)} custom-call(f32[24,80]{1,0:T(8,128)S(1)} %get-tuple-element.64.hot_ref, f32[10,16,80]{2,1,0:T(8,128)S(1)} %get-tuple-element.65.keep_ref, s32[32,16,128]{2,1,0:T(8,128)S(1)} %all-to-all-done.3.got_ref), custom_call_target="tpu_custom_call" | custom-call | tf_op jit(solution)/shard_map/unpack/pallas_call | solution.py:506
  57.6 0.0 copy-done.2
  57.6 0.0 copy-done.4
  (1 shorter events, 0.0 us)
Async XLA Ops:
  2.6 12.4 %all-to-all-start.2 = ((bf16[8,24,512]{2,1,0:T(8,128)(2,1)}), bf16[8,24,512]{2,1,0:T(8,128)(2,1)S(1)}, u32[]{:S(2)}, u32[]{:S(2)}) async-start(bf16[8,24,512]{2,1,0:T(8,128)(2,1)} %pack.2), calls=%async_computation.2 | async-start | bytes 393216 | tf_op jit(solution)/shard_map/all_to_all | solution.py:452
  17.5 3.3 %collective-permute-start.4 = (s32[96,2688]{1,0:T(8,128)S(1)}, s32[96,2688]{1,0:T(8,128)S(1)}, u32[]{:S(2)}, u32[]{:S(2)}) collective-permute-start(s32[96,2688]{1,0:T(8,128)S(1)} %send_rows.2), channel_id=1, source_target_pairs={{0,32},{32,0},{64,96},{96,64},{128,160},{160,128},{192,224},{224,1... | collective-permute-start | bytes 3096584 | tf_op jit(solution)/shard_map/ppermute | solution.py:467
  20.1 24.7 %copy-start.3 = (s32[640]{0:T(1024)S(1)}, s32[640]{0:T(1024)}, u32[]{:S(2)}) copy-start(s32[640]{0:T(1024)} %pairs_v.3) | copy-start | bytes 7684
  20.1 37.5 %copy-start.2 = (s32[320]{0:T(512)S(1)}, s32[320]{0:T(512)}, u32[]{:S(2)}) copy-start(s32[320]{0:T(512)} %virt_v.3) | copy-start | bytes 3844
  20.2 37.5 %copy-start.4 = (s32[16]{0:T(128)S(1)}, s32[16]{0:T(128)}, u32[]{:S(2)}) copy-start(s32[16]{0:T(128)} %tile_s.1) | copy-start | bytes 196
  22.4 6.8 %collective-permute-start.5 = (s32[504,128]{1,0:T(8,128)S(1)}, s32[504,128]{1,0:T(8,128)S(1)}, u32[]{:S(2)}, u32[]{:S(2)}) collective-permute-start(s32[504,128]{1,0:T(8,128)S(1)} %get-tuple-element.69), channel_id=1, source_target_pairs={{0,64},{32,40},{1,65},{33,41},{2,66},{34,42},{3,67},{35,43},{4,68}... | collective-permute-start | bytes 774152 | tf_op jit(solution)/shard_map/ppermute | solution.py:492
  23.0 8.2 %collective-permute-start.6 = (s32[504,128]{1,0:T(8,128)S(1)}, s32[504,128]{1,0:T(8,128)S(1)}, u32[]{:S(2)}, u32[]{:S(2)}) collective-permute-start(s32[504,128]{1,0:T(8,128)S(1)} %get-tuple-element.70), channel_id=1, source_target_pairs={{0,192},{32,56},{1,193},{33,57},{2,194},{34,58},{3,195},{35,59},{4... | collective-permute-start | bytes 774152 | tf_op jit(solution)/shard_map/ppermute | solution.py:492
  25.1 7.3 %collective-permute-start.7 = (s32[504,128]{1,0:T(8,128)S(1)}, s32[504,128]{1,0:T(8,128)S(1)}, u32[]{:S(2)}, u32[]{:S(2)}) collective-permute-start(s32[504,128]{1,0:T(8,128)S(1)} %get-tuple-element.71), channel_id=1, source_target_pairs={{0,128},{32,48},{1,129},{33,49},{2,130},{34,50},{3,131},{35,51},{4... | collective-permute-start | bytes 774152 | tf_op jit(solution)/shard_map/ppermute | solution.py:492
  34.5 21.8 %all-to-all-start.3 = ((s32[32,16,128]{2,1,0:T(8,128)}), s32[32,16,128]{2,1,0:T(8,128)S(1)}, u32[]{:S(2)}, u32[]{:S(2)}) async-start(s32[32,16,128]{2,1,0:T(8,128)} %column_sum.2), calls=%async_computation.3 | async-start | bytes 524288 | tf_op jit(solution)/shard_map/all_to_all | solution.py:503

commit v5 on v4

--- a/solution.py
+++ b/solution.py
@@ -123,7 +123,7 @@
         return pltpu.make_async_copy(int_hbm.at[c], slabs.at[c], sems.at[c])
 
     def save(step):
-        rows = pl.ds(pl.multiple_of(step * 2 * OWN_D, 16), 2 * OWN_D)
+        rows = pl.ds(step * 2 * OWN_D, 2 * OWN_D)
         return pltpu.make_async_copy(far.at[:, rows, :], far_hbm.at[:, rows, :], far_sems.at[step])
 
     for c in range(OWN_C):
@@ -144,8 +144,8 @@
     base_c = lax.axis_index("virt") * OWN_C
     base_d = lax.axis_index("pair") * OWN_D
 
-    @pl.loop(0, OWN_C // 2)
-    def _(step):
+    for step in range(OWN_C // 2):
+        buffer = wide.at[step % 2]
         load(step * 2).wait()
         load(step * 2 + 1).wait()
         for group in range(GROUPS):
@@ -153,11 +153,11 @@
                 c, d = divmod(group * 16 + k, OWN_D)
                 g = jnp.bitwise_xor(virt_s[base_c + step * 2 + c], virt_s[base_d + d])
                 start = group * WIDTH_PAD
-                wide[k * 16 : (k + 1) * 16, start : start + WIDTH] = slabs[step * 2 + c, d] * masks[g]
-        turned = jnp.dot(turn[...], wide[...], preferred_element_type=F32).astype(BF16)
+                buffer[k * 16 : (k + 1) * 16, start : start + WIDTH] = slabs[step * 2 + c, d] * masks[g]
+        turned = jnp.dot(turn[...], buffer[...], preferred_element_type=F32).astype(BF16)
         for group in range(GROUPS):
             start = group * WIDTH_PAD
-            rows = pl.ds(pl.multiple_of(step * 2 * OWN_D + group * 16, 16), 16)
+            rows = pl.ds(step * 2 * OWN_D + group * 16, 16)
             for b in range(TILE):
                 pair, side = divmod(b, 2)
                 out, at = (near_ref, pair) if pair < NEAR else (far, pair - NEAR)
@@ -166,8 +166,7 @@
                 ]
         save(step).start()
 
-    @pl.loop(0, OWN_C // 2)
-    def _(step):
+    for step in range(OWN_C // 2):
         save(step).wait()
 
 
@@ -267,7 +266,7 @@
     return cuts
 
 
-def chip_kernel(keep_ref, got_ref, own_ref, one_ref, three_ref, two_ref, values, words, spread):
+def chip_kernel(keep_ref, got_ref, own_ref, one_ref, three_ref, two_ref, values, words):
     core = lax.axis_index("pair") % CORES
     outs = (own_ref, one_ref, two_ref, three_ref)
     top = add_words(got_ref, values, keep_ref)
@@ -287,17 +286,21 @@
         lane = iota((SLOTS, 128), 1)
         codes = [words[q * SLOTS : (q + 1) * SLOTS, WORDS:MESSAGE] for q in range(CHIPS)]
         tail = jnp.where(lane == 0, codes[0], jnp.where(lane == 1, codes[1], jnp.where(lane == 2, codes[2], codes[3])))
+        here = lax.axis_index("virt") // LAYERS
         for y in range(CHIPS):
-            for b in range(HALF):
-                for at, tile, to, size in crossing(b * own_width, own_width):
-                    start = b * WIDTH + y * own_width + at
-                    spread[y, tile * CORE_ROWS : (tile + 1) * CORE_ROWS, to : to + size] = words[
-                        :, start : start + size
-                    ]
-            spread[y, TILES * SLOTS : BLOCK, :] = tail
-        here = lax.axis_index("virt") // LAYERS
-        for hop, out in enumerate(outs):
-            out[...] = spread[lax.rem(here + hop, CHIPS)]
+
+            @pl.when(here == y)
+            def _():
+                for hop, out in enumerate(outs):
+                    for b in range(HALF):
+                        for at, tile, to, size in crossing(b * own_width, own_width):
+                            start = b * WIDTH + (y + hop) % CHIPS * own_width + at
+                            out[tile * CORE_ROWS : (tile + 1) * CORE_ROWS, to : to + size] = words[
+                                :, start : start + size
+                            ]
+
+        for out in outs:
+            out[TILES * SLOTS : BLOCK, :] = tail
 
 
 def piece(group, b):
@@ -424,7 +427,7 @@
             pltpu.VMEM((OWN_C, OWN_D, TILE, WIDTH), BF16),
             pltpu.VMEM((8, TILE, WIDTH), BF16),
             pltpu.VMEM((256, 256), BF16),
-            pltpu.VMEM((256, GROUPS * WIDTH_PAD), BF16),
+            pltpu.VMEM((2, 256, GROUPS * WIDTH_PAD), BF16),
             pltpu.VMEM((FAR, DEPTH, PAIR), BF16),
             pltpu.SemaphoreType.DMA((OWN_C,)),
             pltpu.SemaphoreType.DMA((OWN_C // 2,)),
@@ -483,7 +486,6 @@
         scratch_shapes=[
             table,
             pltpu.VMEM((CORE_ROWS, MESSAGE), I32),
-            pltpu.VMEM((CHIPS, BLOCK, 128), I32),
         ],
         compiler_params=params(),
         name="chip_sum",

time: 58.1 us -> 57.9 us (level)
  the two profiles are of different devices: /device:TPU:1 before, /device:TPU:6 now
where the time goes in v5:
time: 57.9 us; the launch traced here: 56.9 us
  starting transfers between devices  20 us (35%)
  waiting for transfers between devices  18.4 us (32%)
  Pallas kernels  16.7 us (29%)
  other arithmetic  0.85 us (1%)
  between operations  0.77 us (1%)
    all_to_all x1, starting transfers between devices, one_round(): lax.all_to_all(parts, ('pair', 'virt'), split_axis=0, concat_axis=0, tile...  10.7 us
    all_to_all x1, waiting for transfers between devices, one_round(): lax.all_to_all(parts, ('pair', 'virt'), split_axis=0, concat_axis=0, tile...  9.7 us
    ppermute x3, waiting for transfers between devices, one_round(): lax.ppermute(part, ('pair', 'virt'), hop_pairs(hop))  7.88 us
    pallas_call x1, Pallas kernels, masked_integrals(): pl.pallas_call(mask_kernel, out_shape=[pltpu.VMEM((NEAR, DEPTH, PAIR), BF...  5.78 us
    all_to_all x1, starting transfers between devices, one_round(): lax.all_to_all(packed, 'pair', split_axis=0, concat_axis=0, tiled=True)  5.54 us
    ppermute x3, starting transfers between devices, one_round(): lax.ppermute(part, ('pair', 'virt'), hop_pairs(hop))  3.53 us
    pallas_call x1, Pallas kernels, one_round(): pl.pallas_call(pack_kernel, out_shape=shape((OWNERS, SLOTS, DEPTH_PAD), B...  2.62 us
    pallas_call x1, Pallas kernels, one_round(): pl.pallas_call(send_kernel, out_shape=shape((CORE_ROWS, MESSAGE), I32), i...  2.42 us
  transfers between devices with their start and end apart: 6, of which 4 were waited for; matrix products, arithmetic and copies ran while one was open for 2% of the time, Pallas kernels for 13%

profile of v5, /device:TPU:6, one launch (start us, length us, event | category | flops | bytes accessed | tf_op | source)
XLA Modules:
  0.0 56.9 jit_solution(9539604135974334075)
XLA Ops:
  0.0 2.6 %pack.2 = bf16[8,24,512]{2,1,0:T(8,128)(2,1)} custom-call(s32[1]{0:T(128)} %constant.16.clone.1.round_ref, s32[320]{0:T(512)} %virt_v.3, s32[320]{0:T(512)} %virt_v.3, s32[640]{0:T(1024)} %pairs_v.3, bf16[10,80,320]{2,1,0:T(8,128)(2,1)} %bitcast.8), custom_call_target="tpu_custom_call" | custom-call | tf_op jit(solution)/shard_map/pack/pallas_call | solution.py:443
  2.6 5.5 %all-to-all-start.2 = ((bf16[8,24,512]{2,1,0:T(8,128)(2,1)}), bf16[8,24,512]{2,1,0:T(8,128)(2,1)S(1)}, u32[]{:S(2)}, u32[]{:S(2)}) async-start(bf16[8,24,512]{2,1,0:T(8,128)(2,1)} %pack.2), calls=%async_computation.2 | async-start | bytes 393216 | tf_op jit(solution)/shard_map/all_to_all | solution.py:455
  8.2 5.8 %mask_turn.2 = (bf16[6,400,640]{2,1,0:T(8,128)(2,1)S(1)}, bf16[2,400,640]{2,1,0:T(8,128)(2,1)}, f32[24,80]{1,0:T(8,128)S(1)}, f32[10,16,80]{2,1,0:T(8,128)S(1)}) custom-call(s32[1]{0:T(128)} %constant.16.clone.1.round_ref, s32[320]{0:T(512)} %virt_v.3, s32[16]{0:T(128)} %tile_s.1, s32[320]{0:T(512)} %virt_v.3, s32[640]{0:T(1024)} %pairs_v.3, ...), custom_call_target="tpu_custom_call" | custom-call | flops 1073741824 | bytes 10485760 | tf_op jit(solution)/shard_map/mask_turn/pallas_call | solution.py:416
  13.9 0.0 all-to-all-done.2.amp_ref
  14.0 2.4 %send_rows.2 = s32[96,2688]{1,0:T(8,128)S(1)} custom-call(bf16[8,24,512]{2,1,0:T(8,128)(2,1)S(1)} %all-to-all-done.2.amp_ref, bf16[6,400,640]{2,1,0:T(8,128)(2,1)S(1)} %get-tuple-element.66.near_ref, bf16[2,400,640]{2,1,0:T(8,128)(2,1)} %get-tuple-element.67.far_hbm), custom_call_target="tpu_custom_call" | custom-call | tf_op jit(solution)/shard_map/send_rows/pallas_call | solution.py:461
  16.4 0.2 collective-permute-start.4
  16.6 1.6 %keep_rows.2.keep_ref = f32[8,96,640]{2,1,0:T(8,128)S(1)} custom-call(bf16[8,24,512]{2,1,0:T(8,128)(2,1)S(1)} %all-to-all-done.2.amp_ref, bf16[6,400,640]{2,1,0:T(8,128)(2,1)S(1)} %get-tuple-element.66.near_ref, bf16[2,400,640]{2,1,0:T(8,128)(2,1)} %get-tuple-element.67.far_hbm), custom_call_target="tpu_custom_call" | custom-call | flops 536870912 | bytes 8388608 | tf_op jit(solution)/shard_map/keep_rows/pallas_call | solution.py:471
  18.2 0.0 copy-start.3
  18.2 0.0 copy-start.2
  18.2 0.0 copy-start.4
  18.2 0.9 %collective-permute-done.4.got_ref = s32[96,2688]{1,0:T(8,128)S(1)} collective-permute-done((s32[96,2688]{1,0:T(8,128)S(1)}, s32[96,2688]{1,0:T(8,128)S(1)}, u32[]{:S(2)}, u32[]{:S(2)}) %collective-permute-start.4) | collective-permute-done | bytes 1032224 | tf_op jit(solution)/shard_map/ppermute | solution.py:470
  19.1 0.8 %chip_sum.2 = (s32[504,128]{1,0:T(8,128)S(1)}, s32[504,128]{1,0:T(8,128)S(1)}, s32[504,128]{1,0:T(8,128)S(1)}, s32[504,128]{1,0:T(8,128)S(1)}) custom-call(f32[8,96,640]{2,1,0:T(8,128)S(1)} %keep_rows.2.keep_ref, s32[96,2688]{1,0:T(8,128)S(1)} %collective-permute-done.4.got_ref), custom_call_target="tpu_custom_call" | custom-call | tf_op jit(solution)/shard_map/chip_sum/pallas_call | solution.py:481
  19.9 1.1 %collective-permute-start.5 = (s32[504,128]{1,0:T(8,128)S(1)}, s32[504,128]{1,0:T(8,128)S(1)}, u32[]{:S(2)}, u32[]{:S(2)}) collective-permute-start(s32[504,128]{1,0:T(8,128)S(1)} %get-tuple-element.69), channel_id=1, source_target_pairs={{0,64},{32,40},{1,65},{33,41},{2,66},{34,42},{3,67},{35,43},{4,68}... | collective-permute-start | bytes 774152 | tf_op jit(solution)/shard_map/ppermute | solution.py:494
  21.0 1.0 %collective-permute-start.6 = (s32[504,128]{1,0:T(8,128)S(1)}, s32[504,128]{1,0:T(8,128)S(1)}, u32[]{:S(2)}, u32[]{:S(2)}) collective-permute-start(s32[504,128]{1,0:T(8,128)S(1)} %get-tuple-element.70), channel_id=1, source_target_pairs={{0,192},{32,56},{1,193},{33,57},{2,194},{34,58},{3,195},{35,59},{4... | collective-permute-start | bytes 774152 | tf_op jit(solution)/shard_map/ppermute | solution.py:494
  22.0 1.4 %collective-permute-start.7 = (s32[504,128]{1,0:T(8,128)S(1)}, s32[504,128]{1,0:T(8,128)S(1)}, u32[]{:S(2)}, u32[]{:S(2)}) collective-permute-start(s32[504,128]{1,0:T(8,128)S(1)} %get-tuple-element.71), channel_id=1, source_target_pairs={{0,128},{32,48},{1,129},{33,49},{2,130},{34,50},{3,131},{35,51},{4... | collective-permute-start | bytes 774152 | tf_op jit(solution)/shard_map/ppermute | solution.py:494
  23.4 2.9 %collective-permute-done.5.one_ref = s32[504,128]{1,0:T(8,128)S(1)} collective-permute-done((s32[504,128]{1,0:T(8,128)S(1)}, s32[504,128]{1,0:T(8,128)S(1)}, u32[]{:S(2)}, u32[]{:S(2)}) %collective-permute-start.5) | collective-permute-done | bytes 258080 | tf_op jit(solution)/shard_map/ppermute | solution.py:494
  26.3 5.0 %collective-permute-done.6.three_ref = s32[504,128]{1,0:T(8,128)S(1)} collective-permute-done((s32[504,128]{1,0:T(8,128)S(1)}, s32[504,128]{1,0:T(8,128)S(1)}, u32[]{:S(2)}, u32[]{:S(2)}) %collective-permute-start.6) | collective-permute-done | bytes 258080 | tf_op jit(solution)/shard_map/ppermute | solution.py:494
  31.3 0.0 collective-permute-done.7.two_ref
  31.3 2.3 %column_sum.2 = s32[32,16,128]{2,1,0:T(8,128)} custom-call(s32[504,128]{1,0:T(8,128)S(1)} %get-tuple-element.68.own_ref, s32[504,128]{1,0:T(8,128)S(1)} %collective-permute-done.5.one_ref, s32[504,128]{1,0:T(8,128)S(1)} %collective-permute-done.6.three_ref, s32[504,128]{1,0:T(8,128)S(1)} %collective-permute-done.7.two_ref), custom_call_target="tpu_custom_call" | custom-call | tf_op jit(solution)/shard_map/column_sum/pallas_call | solution.py:496
  33.5 10.7 %all-to-all-start.3 = ((s32[32,16,128]{2,1,0:T(8,128)}), s32[32,16,128]{2,1,0:T(8,128)S(1)}, u32[]{:S(2)}, u32[]{:S(2)}) async-start(s32[32,16,128]{2,1,0:T(8,128)} %column_sum.2), calls=%async_computation.3 | async-start | bytes 524288 | tf_op jit(solution)/shard_map/all_to_all | solution.py:505
  44.3 0.0 copy-done.3
  44.3 0.1 eq.15
  44.4 0.2 convert_reduce_fusion
  44.6 0.6 %reduce_max.9 = s32[]{:T(128)} reduce(s32[8,8]{1,0:T(8,128)S(1)} %convert_reduce_fusion, s32[]{:T(128)} %constant.18.clone.1), dimensions={0,1}, to_apply=%region_1.0 | reduce | flops 63 | bytes 264 | tf_op jit(solution)/shard_map/reduce_max | solution.py:531
  45.9 9.7 %all-to-all-done.3.got_ref = s32[32,16,128]{2,1,0:T(8,128)S(1)} async-done(((s32[32,16,128]{2,1,0:T(8,128)}), s32[32,16,128]{2,1,0:T(8,128)S(1)}, u32[]{:S(2)}, u32[]{:S(2)}) %all-to-all-start.3) | async-done | bytes 262176 | tf_op jit(solution)/shard_map/all_to_all | solution.py:505
  55.6 1.3 %unpack.2 = f32[10,16,80]{2,1,0:T(8,128)} custom-call(f32[24,80]{1,0:T(8,128)S(1)} %get-tuple-element.64.hot_ref, f32[10,16,80]{2,1,0:T(8,128)S(1)} %get-tuple-element.65.keep_ref, s32[32,16,128]{2,1,0:T(8,128)S(1)} %all-to-all-done.3.got_ref), custom_call_target="tpu_custom_call" | custom-call | tf_op jit(solution)/shard_map/unpack/pallas_call | solution.py:508
  56.9 0.0 copy-done.2
  56.9 0.0 copy-done.4
  (1 shorter events, 0.0 us)
Async XLA Ops:
  2.6 11.3 %all-to-all-start.2 = ((bf16[8,24,512]{2,1,0:T(8,128)(2,1)}), bf16[8,24,512]{2,1,0:T(8,128)(2,1)S(1)}, u32[]{:S(2)}, u32[]{:S(2)}) async-start(bf16[8,24,512]{2,1,0:T(8,128)(2,1)} %pack.2), calls=%async_computation.2 | async-start | bytes 393216 | tf_op jit(solution)/shard_map/all_to_all | solution.py:455
  16.4 2.7 %collective-permute-start.4 = (s32[96,2688]{1,0:T(8,128)S(1)}, s32[96,2688]{1,0:T(8,128)S(1)}, u32[]{:S(2)}, u32[]{:S(2)}) collective-permute-start(s32[96,2688]{1,0:T(8,128)S(1)} %send_rows.2), channel_id=1, source_target_pairs={{0,32},{32,0},{64,96},{96,64},{128,160},{160,128},{192,224},{224,1... | collective-permute-start | bytes 3096584 | tf_op jit(solution)/shard_map/ppermute | solution.py:470
  18.2 26.1 %copy-start.3 = (s32[640]{0:T(1024)S(1)}, s32[640]{0:T(1024)}, u32[]{:S(2)}) copy-start(s32[640]{0:T(1024)} %pairs_v.3) | copy-start | bytes 7684
  18.2 38.7 %copy-start.2 = (s32[320]{0:T(512)S(1)}, s32[320]{0:T(512)}, u32[]{:S(2)}) copy-start(s32[320]{0:T(512)} %virt_v.3) | copy-start | bytes 3844
  18.2 38.7 %copy-start.4 = (s32[16]{0:T(128)S(1)}, s32[16]{0:T(128)}, u32[]{:S(2)}) copy-start(s32[16]{0:T(128)} %tile_s.1) | copy-start | bytes 196
  19.9 6.4 %collective-permute-start.5 = (s32[504,128]{1,0:T(8,128)S(1)}, s32[504,128]{1,0:T(8,128)S(1)}, u32[]{:S(2)}, u32[]{:S(2)}) collective-permute-start(s32[504,128]{1,0:T(8,128)S(1)} %get-tuple-element.69), channel_id=1, source_target_pairs={{0,64},{32,40},{1,65},{33,41},{2,66},{34,42},{3,67},{35,43},{4,68}... | collective-permute-start | bytes 774152 | tf_op jit(solution)/shard_map/ppermute | solution.py:494
  21.0 10.3 %collective-permute-start.6 = (s32[504,128]{1,0:T(8,128)S(1)}, s32[504,128]{1,0:T(8,128)S(1)}, u32[]{:S(2)}, u32[]{:S(2)}) collective-permute-start(s32[504,128]{1,0:T(8,128)S(1)} %get-tuple-element.70), channel_id=1, source_target_pairs={{0,192},{32,56},{1,193},{33,57},{2,194},{34,58},{3,195},{35,59},{4... | collective-permute-start | bytes 774152 | tf_op jit(solution)/shard_map/ppermute | solution.py:494
  22.0 9.3 %collective-permute-start.7 = (s32[504,128]{1,0:T(8,128)S(1)}, s32[504,128]{1,0:T(8,128)S(1)}, u32[]{:S(2)}, u32[]{:S(2)}) collective-permute-start(s32[504,128]{1,0:T(8,128)S(1)} %get-tuple-element.71), channel_id=1, source_target_pairs={{0,128},{32,48},{1,129},{33,49},{2,130},{34,50},{3,131},{35,51},{4... | collective-permute-start | bytes 774152 | tf_op jit(solution)/shard_map/ppermute | solution.py:494
  33.5 22.1 %all-to-all-start.3 = ((s32[32,16,128]{2,1,0:T(8,128)}), s32[32,16,128]{2,1,0:T(8,128)S(1)}, u32[]{:S(2)}, u32[]{:S(2)}) async-start(s32[32,16,128]{2,1,0:T(8,128)} %column_sum.2), calls=%async_computation.3 | async-start | bytes 524288 | tf_op jit(solution)/shard_map/all_to_all | solution.py:505
